TPU v7x, 32 devices: a whole 2x2x4 slice. The times are simulated.
32 devices in a mesh: ctx: 16 (over z, x, core), head: 2 (over y).
Axes of the slice: x: 2, y: 2, z: 4, core: 2. Of those that a mesh axis runs over, the one named last changes fastest.
Arguments:
- kv_latent: bfloat16 [8192, 576], P('ctx'), may hold values from -4 to 4
- queries: bfloat16 [8192, 3072], P('ctx', 'head'), may hold values from -22 to 22
- grad_out: bfloat16 [8192, 2048], P('ctx', 'head'), may hold values from -6 to 6
- kv_up_weight: bfloat16 [512, 4096], P(None, 'head'), may hold values from -0.25 to 0.25
- doc_ids: int32 [8192], replicated, may hold values from 0 to 7, never falling along the last dimension, each value on 1 to 1536 neighbouring positions
Outputs:
- grad_queries: bfloat16 [8192, 3072], P('ctx', 'head')
- grad_latent: bfloat16 [8192, 576], P('ctx')
- grad_weight: float32 [512, 4096], P('ctx', 'head')
Inputs may be any that keep to these rules, and one draw needn't show every extreme that they name: `doc_ids`: document ids never fall along the sequence; every document has 1 to 1536 tokens, and one has exactly 1536.
All inputs are finite; a program needn't handle non-finite values.
Results may differ from a plain program's by a relative error of at most 0.0076.
Values may be sent and summed in bfloat16 or wider, within the bound.
No kernel may reach another device: no remote copies, remote signals or barrier semaphores. Data moves between devices by JAX's collectives and lax.ppermute only.
A program may use at most 128 MiB of HBM per device.

v0:
```python
import functools
import math

import jax
import jax.numpy as jnp
from jax import lax
from jax.experimental import pallas as pl
from jax.experimental.pallas import tpu as pltpu
from jax.sharding import PartitionSpec as P

NOPE = 128
ROPE = 64
VDIM = 128
LATENT = 512
REACH = 3
QK = NOPE + ROPE
KV = NOPE + VDIM
WIDTH = LATENT + ROPE
TILE = 256
GROUPS = 2

MASKED = -1e30
FLOOR = -1e20
SCALE = 1.0 / math.sqrt(QK)
SCALE2 = SCALE * math.log2(math.e)

NT = (((1,), (1,)), ((), ()))
NN = (((1,), (0,)), ((), ()))


def dot(a, b, dims=NN):
    return lax.dot_general(a, b, dims, preferred_element_type=jnp.float32)


def attention_kernel(rows, ranks, initial, final, *refs):
    index_ref, docs_sref, docs_ref, q_ref, do_ref, w_ref, lat0, lat1, lat2, lat3, *refs = refs
    if not initial:
        _, x_in, *refs = refs
    dq_ref, keep_ref, send_ref, *refs = refs
    x_outs, refs = (refs[: REACH + 1], refs[REACH + 1 :]) if final else (refs[:1], refs[1:])
    (lat_ref, lat_t_ref, bias_ref, e_ref, g_ref, k_ref, top_ref, dq_acc, gw_acc, x_acc, r_acc,
     sems, x_sem) = refs

    step = pl.program_id(0)
    index = index_ref[0]
    odd = lax.rem(index, 2)
    first_row = index * rows
    tiles_block = rows // TILE
    tiles = (REACH + 1) * tiles_block
    first_doc = docs_sref[first_row]

    def window_base(t):
        block = t // tiles_block
        base = jnp.where(block == 1, rows, REACH * rows)
        base = jnp.where(block == 0, rows * 2 * (1 - odd), base)
        base = jnp.where(block == 2, rows * 2 * odd, base)
        return base + lax.rem(t, tiles_block) * TILE

    def active(t):
        position = first_row - REACH * rows + window_base(t)
        last_doc = docs_sref[jnp.maximum(position, 0) + TILE - 1]
        return (position >= 0) & (last_doc >= first_doc)

    def tile_rows(t):
        return pl.ds(pl.multiple_of(t * TILE, TILE), TILE)

    @pl.when(step == 0)
    def _():
        copies = [
            pltpu.make_async_copy(source, lat_t_ref.at[:, pl.ds(i * rows, rows)], sems.at[i])
            for i, source in enumerate((lat0, lat1, lat2, lat3))
        ]
        for copy in copies:
            copy.start()
        if initial:
            x_acc[...] = jnp.zeros_like(x_acc)
        else:
            x_copy = pltpu.make_async_copy(x_in, x_acc, x_sem)
            x_copy.start()
        r_acc[...] = jnp.zeros_like(r_acc)
        my_docs = docs_ref[:, pl.ds(pl.multiple_of(first_row, rows), rows)]
        last_seen = REACH * rows + lax.broadcasted_iota(jnp.int32, (1, rows), 1)

        def fill(t, carry):
            @pl.when(active(t))
            def _():
                base = window_base(t)
                position = pl.multiple_of(first_row - REACH * rows + base, TILE)
                key_docs = docs_ref[:, pl.ds(position, TILE)]
                key_docs = jnp.broadcast_to(key_docs, (128, TILE)).T[:, :1]
                key = lax.broadcasted_iota(jnp.int32, (TILE, rows), 0)
                seen = (key_docs == my_docs) & (key <= last_seen - base)
                bias_ref[tile_rows(t), :] = jnp.where(seen, 0.0, MASKED)

            return carry

        lax.fori_loop(0, tiles, fill, 0)
        for copy in copies:
            copy.wait()
        for i in range(REACH + 1):
            part = slice(i * rows, (i + 1) * rows)
            lat_ref[part, :] = lat_t_ref[:, part].T
        if not initial:
            x_copy.wait()

    gw_acc[...] = jnp.zeros_like(gw_acc)
    dq_acc[...] = jnp.zeros_like(dq_acc)
    heads = range(2)
    q = [q_ref[:, h * QK : (h + 1) * QK] for h in heads]
    do = [do_ref[:, h * VDIM : (h + 1) * VDIM] for h in heads]

    def first_pass(t, carry):
        def run(carry):
            part = tile_rows(t)
            latent = lat_ref[part, :LATENT]
            rope = lat_ref[part, LATENT:]
            bias = bias_ref[part, :]
            out = []
            for h in heads:
                top, mass, cross = carry[h]
                lifted = dot(latent, w_ref[:, h * KV : (h + 1) * KV]).astype(jnp.bfloat16)
                key = jnp.concatenate([lifted[:, :NOPE], rope], axis=1)
                k_ref[h, part, :] = key
                scores = dot(key, q[h], NT) * SCALE2 + bias
                grads = dot(lifted[:, NOPE:], do[h], NT)
                new_top = jnp.maximum(top, jnp.max(scores, axis=0, keepdims=True))
                weights = jnp.exp2(scores - new_top)
                factor = jnp.exp2(top - new_top)
                mass = mass * factor + jnp.sum(weights, axis=0, keepdims=True)
                cross = cross * factor + jnp.sum(weights * grads, axis=0, keepdims=True)
                e_ref[h, part, :] = weights
                g_ref[h, part, :] = grads
                top_ref[h, pl.ds(t, 1), :] = new_top
                out.append((new_top, mass, cross))
            return tuple(out)

        return lax.cond(active(t), run, lambda c: c, carry)

    zero = jnp.zeros((1, rows), jnp.float32)
    stats = lax.fori_loop(0, tiles, first_pass, ((zero + FLOOR, zero, zero),) * 2)
    inverse = [1.0 / mass for _, mass, _ in stats]
    delta = [cross * inv for (_, _, cross), inv in zip(stats, inverse)]

    def second_pass(t, carry):
        @pl.when(active(t))
        def _():
            part = tile_rows(t)
            pieces = []
            for h in heads:
                factor = jnp.exp2(top_ref[h, pl.ds(t, 1), :] - stats[h][0]) * inverse[h]
                probs = e_ref[h, part, :] * factor
                low = probs.astype(jnp.bfloat16)
                dscore = (probs * (g_ref[h, part, :] - delta[h])).astype(jnp.bfloat16)
                dvalue = dot(low, do[h])
                dkey = dot(dscore, q[h]) * SCALE
                own = slice(h * QK, (h + 1) * QK)
                dq_acc[own, :] += dot(k_ref[h, part, :].T, dscore)
                r_acc[part, :] += dkey[:, NOPE:]
                pieces += [dkey[:, :NOPE].astype(jnp.bfloat16), dvalue.astype(jnp.bfloat16)]
            grads = jnp.concatenate(pieces, axis=1)
            x_acc[:LATENT, part] += dot(w_ref[...], grads, NT)
            gw_acc[...] += dot(lat_t_ref[:LATENT, part], grads)

        return carry

    lax.fori_loop(0, tiles, second_pass, 0)
    dq_ref[...] = (dq_acc[...] * SCALE).T.astype(dq_ref.dtype)
    share = LATENT // ranks
    for i in range(ranks // 2):
        for out, half in ((keep_ref, odd), (send_ref, 1 - odd)):
            source = pl.multiple_of(2 * i * share + half * share, share)
            out[i * share : (i + 1) * share, :] = gw_acc[pl.ds(source, share), :].astype(out.dtype)

    @pl.when(step == pl.num_programs(0) - 1)
    def _():
        x_acc[LATENT:, :] += r_acc[...].T
        if final:
            for i, out in enumerate(x_outs):
                out[...] = x_acc[:, i * rows : (i + 1) * rows].astype(out.dtype)
        else:
            x_copy = pltpu.make_async_copy(x_acc, x_outs[0], x_sem)
            x_copy.start()
            x_copy.wait()


def attention(index, doc_ids, queries, grad_out, weight, blocks, state, group, groups, ranks):
    rows = queries.shape[0]
    heads = weight.shape[1] // KV
    pairs = heads // 2 // groups
    first = group * pairs
    window = (REACH + 1) * rows
    low, full = jnp.bfloat16, jnp.float32
    initial, final = group == 0, group == groups - 1
    anywhere = pl.BlockSpec(memory_space=pl.ANY)
    scalars = pl.BlockSpec(memory_space=pltpu.SMEM)

    def pair_cols(height, size):
        return pl.BlockSpec((height, 2 * size), lambda i: (0, first + i))

    half = pl.BlockSpec((LATENT // 2, 2 * KV), lambda i: (0, i))
    half_shape = jax.ShapeDtypeStruct((LATENT // 2, pairs * 2 * KV), low)
    flops = 2 * pairs * 2 * rows * window * (3 * QK + 2 * VDIM) * 2
    return pl.pallas_call(
        functools.partial(attention_kernel, rows, ranks, initial, final),
        grid=(pairs,),
        in_specs=[
            scalars,
            scalars,
            pl.BlockSpec((1, doc_ids.shape[0]), lambda i: (0, 0)),
            pair_cols(rows, QK),
            pair_cols(rows, VDIM),
            pair_cols(LATENT, KV),
        ]
        + [anywhere] * (REACH + 1 + len(state)),
        out_specs=[pair_cols(rows, QK), half, half]
        + ([pl.BlockSpec((WIDTH, rows), lambda i: (0, 0))] * (REACH + 1) if final else [anywhere]),
        out_shape=[jax.ShapeDtypeStruct(queries.shape, low), half_shape, half_shape]
        + (
            [jax.ShapeDtypeStruct((WIDTH, rows), low)] * (REACH + 1)
            if final
            else [jax.ShapeDtypeStruct((WIDTH, window), full)]
        ),
        input_output_aliases={} if initial else {6 + REACH + 1: 0},
        scratch_shapes=[
            pltpu.VMEM((window, WIDTH), low),
            pltpu.VMEM((WIDTH, window), low),
            pltpu.VMEM((window, rows), full),
            pltpu.VMEM((2, window, rows), full),
            pltpu.VMEM((2, window, rows), full),
            pltpu.VMEM((2, window, QK), low),
            pltpu.VMEM((2, window // TILE, rows), full),
            pltpu.VMEM((2 * QK, rows), full),
            pltpu.VMEM((LATENT, 2 * KV), full),
            pltpu.VMEM((WIDTH, window), full),
            pltpu.VMEM((window, ROPE), full),
            pltpu.SemaphoreType.DMA((REACH + 1,)),
            pltpu.SemaphoreType.DMA,
        ],
        compiler_params=pltpu.CompilerParams(
            dimension_semantics=("arbitrary",), vmem_limit_bytes=56 * 1024 * 1024
        ),
        cost_estimate=pl.CostEstimate(
            flops=flops, bytes_accessed=16 * 1024 * 1024, transcendentals=0
        ),
        name="attention",
    )(index, doc_ids, doc_ids[None], queries, grad_out, weight, *blocks, *state)


def permute(value, axis, target):
    count = lax.axis_size(axis)
    pairs = [(s, target(s)) for s in range(count) if 0 <= target(s) < count]
    return lax.ppermute(value, axis, pairs)


def local(kv_latent, queries, grad_out, kv_up_weight, doc_ids):
    ranks = lax.axis_size("ctx")
    index = lax.axis_index("ctx").astype(jnp.int32)[None]
    low, full = jnp.bfloat16, jnp.float32

    latent = kv_latent.T
    far = permute(latent, "ctx", lambda s: s + 2)
    mixed = permute(latent, "ctx", lambda s: s + 3 if s % 2 else s + 1)
    swapped = permute(far, "ctx", lambda s: s ^ 1)
    blocks = (swapped, far, mixed, latent)

    groups = min(GROUPS, kv_up_weight.shape[1] // (2 * KV))
    chips = [list(range(parity, ranks, 2)) for parity in range(2)]
    state, grad_weight = (), []
    for group in range(groups):
        grad_queries, keep, send, *parts = attention(
            index, doc_ids, queries, grad_out, kv_up_weight, blocks, state, group, groups, ranks
        )
        both = keep.astype(full) + permute(send, "ctx", lambda s: s ^ 1).astype(full)
        both = both.astype(low)
        if group < groups - 1:
            both, *parts = lax.optimization_barrier((both, *parts))
        state = (grad_queries, *parts)
        grad_weight.append(
            lax.psum_scatter(
                both, "ctx", scatter_dimension=0, axis_index_groups=chips, tiled=True
            ).astype(full)
        )

    to_swap, to_far, to_mixed, mine = parts
    from_mixed = permute(to_mixed, "ctx", lambda s: s - 1 if s % 2 else s - 3)
    from_swap = permute(to_swap, "ctx", lambda s: s ^ 1)
    far_sum = (to_far.astype(full) + from_swap.astype(full)).astype(low)
    from_far = permute(far_sum, "ctx", lambda s: s - 2)
    total = mine.astype(full) + from_mixed.astype(full) + from_far.astype(full)
    mine = total.astype(low)
    size = lax.axis_size("head")
    for turn in range(1, size):
        other = lax.ppermute(mine, "head", [(s, (s + turn) % size) for s in range(size)])
        total = total + other.astype(full)
    return grad_queries, total.astype(low).T, jnp.concatenate(grad_weight, axis=1)


def solution(mesh):
    return jax.shard_map(
        local,
        mesh=mesh,
        in_specs=(P("ctx", None), P("ctx", "head"), P("ctx", "head"), P(None, "head"), P()),
        out_specs=(P("ctx", "head"), P("ctx", None), P("ctx", "head")),
        check_vma=False,
    )
```

profile of v0, /device:TPU:0, one launch (start us, length us, event | category | flops | bytes accessed | tf_op | source)
XLA Modules:
  0.0 242.4 jit_solution(1824689047630002774)
XLA Ops:
  7.2 0.0 reduce-scatter.3.cloned.1.call-start
  7.2 4.9 %collective-permute-start = (bf16[576,512]{1,0:T(8,128)(2,1)}, bf16[576,512]{1,0:T(8,128)(2,1)S(1)}, u32[]{:S(2)}, u32[]{:S(2)}) collective-permute-start(bf16[576,512]{1,0:T(8,128)(2,1)} %bitcast.5), channel_id=1, source_target_pairs={{0,4},{2,6},{4,8},{6,10},{8,12},{10,14},{12,16},{14,18},{16,20},{1... | collective-permute-start | bytes 1769480 | tf_op jit(solution)/shard_map/ppermute | solution.py:252
  12.1 1.5 collective-permute-start.2
  13.6 11.3 %collective-permute-done.refs_7_ = bf16[576,512]{1,0:T(8,128)(2,1)S(1)} collective-permute-done((bf16[576,512]{1,0:T(8,128)(2,1)}, bf16[576,512]{1,0:T(8,128)(2,1)S(1)}, u32[]{:S(2)}, u32[]{:S(2)}) %collective-permute-start) | collective-permute-done | bytes 589856 | tf_op jit(solution)/shard_map/ppermute | solution.py:252
  24.9 0.0 copy-start.2
  24.9 0.0 collective-permute-start.1
  25.0 0.0 collective-permute-done.2.refs_8_
  25.0 0.0 copy-start.3
  25.0 2.0 collective-permute-done.1.refs_6_
  27.0 0.0 copy-start.4
  27.0 0.0 copy-done.2
  27.0 0.0 copy-done.3
  27.0 0.8 copy-done.4
  27.8 15.9 %attention.2 = (bf16[512,1536]{1,0:T(8,128)(2,1)}, bf16[256,1024]{1,0:T(8,128)(2,1)}, bf16[256,1024]{1,0:T(8,128)(2,1)}, f32[576,2048]{1,0:T(8,128)}) custom-call(s32[1]{0:T(128)} %bitcast.refs_0_, s32[8192]{0:T(1024)} %refs_1_.3, s32[1,8192]{1,0:T(1,128)} %bitcast.9, bf16[512,1536]{1,0:T(8,128)(2,1)} %refs_3_.3, bf16[512,1024]{1,0:T(8,128)(2,1)} %refs_4_.3, ...), custom_call_target="tpu_custom_call" | custom-call | flops 13958643712 | bytes 16777216 | tf_op jit(solution)/shard_map/attention/pallas_call | solution.py:203
  43.7 7.2 %collective-permute-start.3 = (bf16[256,1024]{1,0:T(8,128)(2,1)}, bf16[256,1024]{1,0:T(8,128)(2,1)S(1)}, u32[]{:S(2)}, u32[]{:S(2)}) collective-permute-start(bf16[256,1024]{1,0:T(8,128)(2,1)} %get-tuple-element.18), channel_id=1, source_target_pairs={{0,2},{2,0},{4,6},{6,4},{8,10},{10,8},{12,14},{14,12},{16,18},{18,... | collective-permute-start | bytes 1572872 | tf_op jit(solution)/shard_map/ppermute | solution.py:252
  50.9 1.7 collective-permute-done.3
  52.6 2.1 add_convert_fusion.3
  54.7 15.5 %attention.3 = (bf16[512,1536]{1,0:T(8,128)(2,1)}, bf16[256,1024]{1,0:T(8,128)(2,1)}, bf16[256,1024]{1,0:T(8,128)(2,1)}, bf16[576,512]{1,0:T(8,128)(2,1)}, bf16[...) custom-call(s32[1]{0:T(128)} %bitcast.refs_0_, ...), custom_call_target="tpu_custom_call", output_to_operand_aliasing={{0}: (10, {})} | custom-call | flops 13958643712 | bytes 16777216 | tf_op jit(solution)/shard_map/attention/pallas_call | solution.py:203
  70.2 0.0 copy-start.1
  70.2 7.4 %collective-permute-start.5 = (bf16[576,512]{1,0:T(8,128)(2,1)}, bf16[576,512]{1,0:T(8,128)(2,1)S(1)}, u32[]{:S(2)}, u32[]{:S(2)}) collective-permute-start(bf16[576,512]{1,0:T(8,128)(2,1)} %get-tuple-element.25), channel_id=1, source_target_pairs={{0,2},{2,0},{4,6},{6,4},{8,10},{10,8},{12,14},{14,12},{16,18},{18,... | collective-permute-start | bytes 1769480 | tf_op jit(solution)/shard_map/ppermute | solution.py:252
  77.6 0.0 reduce-scatter.3.cloned.1.call-update
  77.6 0.0 reduce-scatter.5.cloned.1.call-start
  77.6 0.1 collective-permute-start.8
  77.7 1.3 collective-permute-start.4
  79.0 0.4 collective-permute-done.5
  79.4 1.2 add_convert_fusion.1
  80.6 0.0 copy-start
  80.6 1.4 collective-permute-start.6
  82.1 0.0 collective-permute-done.8
  82.1 0.0 copy-done.1
  82.1 1.0 add_convert_fusion.2
  83.1 0.0 reduce-scatter.5.cloned.1.call-update
  83.1 0.0 collective-permute-done.4
  83.1 30.6 %collective-permute-done.6 = bf16[576,512]{1,0:T(8,128)(2,1)S(1)} collective-permute-done((bf16[576,512]{1,0:T(8,128)(2,1)S(1)}, bf16[576,512]{1,0:T(8,128)(2,1)S(1)}, u32[]{:S(2)}, u32[]{:S(2)}) %collective-permute-start.6) | collective-permute-done | bytes 589856 | tf_op jit(solution)/shard_map/ppermute | solution.py:252
  113.7 0.0 copy-done
  113.7 0.2 fusion
  113.9 1.6 collective-permute-start.7
  115.5 52.1 %reduce-scatter.3.cloned.1.call-done = bf16[32,1024]{1,0:T(8,128)(2,1)} async-done(((bf16[256,1024]{1,0:T(8,128)(2,1)}), bf16[32,1024]{1,0:T(8,128)(2,1)}) %reduce-scatter.3.cloned.1.call-update) | async-done | bytes 65552 | tf_op jit(solution)/shard_map/reduce_scatter | solution.py:279
  167.6 65.3 %reduce-scatter.5.cloned.1.call-done = bf16[32,1024]{1,0:T(8,128)(2,1)} async-done(((bf16[256,1024]{1,0:T(8,128)(2,1)}), bf16[32,1024]{1,0:T(8,128)(2,1)}) %reduce-scatter.5.cloned.1.call-update) | async-done | bytes 65552 | tf_op jit(solution)/shard_map/reduce_scatter | solution.py:279
  232.9 1.6 maximum_convert_fusion
  234.5 0.0 collective-permute-done.7
  234.5 1.1 fusion.1
Async XLA Ops:
  7.2 160.4 %reduce-scatter.3.cloned.1.call-start = ((), (), s32[]{:S(2)}) async-start(), calls=%async_computation.2 | async-start | bytes 589824 | tf_op jit(solution)/shard_map/reduce_scatter | solution.py:279
  7.2 17.7 %collective-permute-start = (bf16[576,512]{1,0:T(8,128)(2,1)}, bf16[576,512]{1,0:T(8,128)(2,1)S(1)}, u32[]{:S(2)}, u32[]{:S(2)}) collective-permute-start(bf16[576,512]{1,0:T(8,128)(2,1)} %bitcast.5), channel_id=1, source_target_pairs={{0,4},{2,6},{4,8},{6,10},{8,12},{10,14},{12,16},{14,18},{16,20},{1... | collective-permute-start | bytes 1769480 | tf_op jit(solution)/shard_map/ppermute | solution.py:252
  12.1 12.9 %collective-permute-start.2 = (bf16[576,512]{1,0:T(8,128)(2,1)}, bf16[576,512]{1,0:T(8,128)(2,1)S(1)}, u32[]{:S(2)}, u32[]{:S(2)}) collective-permute-start(bf16[576,512]{1,0:T(8,128)(2,1)} %bitcast.6), channel_id=1, source_target_pairs={{0,2},{2,8},{4,6},{6,12},{8,10},{10,16},{12,14},{14,20},{16,18},{1... | collective-permute-start | bytes 1769480 | tf_op jit(solution)/shard_map/ppermute | solution.py:252
  24.9 2.0 copy-start.2
  24.9 2.0 collective-permute-start.1
  25.0 2.0 copy-start.3
  27.0 0.8 copy-start.4
  43.7 8.9 %collective-permute-start.3 = (bf16[256,1024]{1,0:T(8,128)(2,1)}, bf16[256,1024]{1,0:T(8,128)(2,1)S(1)}, u32[]{:S(2)}, u32[]{:S(2)}) collective-permute-start(bf16[256,1024]{1,0:T(8,128)(2,1)} %get-tuple-element.18), channel_id=1, source_target_pairs={{0,2},{2,0},{4,6},{6,4},{8,10},{10,8},{12,14},{14,12},{16,18},{18,... | collective-permute-start | bytes 1572872 | tf_op jit(solution)/shard_map/ppermute | solution.py:252
  70.2 11.9 %copy-start.1 = (bf16[256,1024]{1,0:T(8,128)(2,1)S(1)}, bf16[256,1024]{1,0:T(8,128)(2,1)}, u32[]{:S(2)}) copy-start(bf16[256,1024]{1,0:T(8,128)(2,1)} %get-tuple-element.27) | copy-start | bytes 1572868
  70.2 9.2 %collective-permute-start.5 = (bf16[576,512]{1,0:T(8,128)(2,1)}, bf16[576,512]{1,0:T(8,128)(2,1)S(1)}, u32[]{:S(2)}, u32[]{:S(2)}) collective-permute-start(bf16[576,512]{1,0:T(8,128)(2,1)} %get-tuple-element.25), channel_id=1, source_target_pairs={{0,2},{2,0},{4,6},{6,4},{8,10},{10,8},{12,14},{14,12},{16,18},{18,... | collective-permute-start | bytes 1769480 | tf_op jit(solution)/shard_map/ppermute | solution.py:252
  77.6 155.3 %reduce-scatter.5.cloned.1.call-start = ((), (), s32[]{:S(2)}) async-start(), calls=%async_computation.3 | async-start | bytes 589824 | tf_op jit(solution)/shard_map/reduce_scatter | solution.py:279
  77.6 4.4 %collective-permute-start.8 = (bf16[256,1024]{1,0:T(8,128)(2,1)}, bf16[256,1024]{1,0:T(8,128)(2,1)S(1)}, u32[]{:S(2)}, u32[]{:S(2)}) collective-permute-start(bf16[256,1024]{1,0:T(8,128)(2,1)} %get-tuple-element.28), channel_id=1, source_target_pairs={{0,2},{2,0},{4,6},{6,4},{8,10},{10,8},{12,14},{14,12},{16,18},{18,... | collective-permute-start | bytes 1572872 | tf_op jit(solution)/shard_map/ppermute | solution.py:252
  77.7 5.4 %collective-permute-start.4 = (bf16[576,512]{1,0:T(8,128)(2,1)}, bf16[576,512]{1,0:T(8,128)(2,1)S(1)}, u32[]{:S(2)}, u32[]{:S(2)}) collective-permute-start(bf16[576,512]{1,0:T(8,128)(2,1)} %get-tuple-element.23), channel_id=1, source_target_pairs={{2,0},{6,4},{8,2},{10,8},{12,6},{14,12},{16,10},{18,16},{20,14},{2... | collective-permute-start | bytes 1769480 | tf_op jit(solution)/shard_map/ppermute | solution.py:252
  80.6 33.1 %copy-start = (bf16[576,512]{1,0:T(8,128)(2,1)S(1)}, bf16[576,512]{1,0:T(8,128)(2,1)}, u32[]{:S(2)}) copy-start(bf16[576,512]{1,0:T(8,128)(2,1)} %get-tuple-element.22) | copy-start | bytes 1769476
  80.6 33.0 %collective-permute-start.6 = (bf16[576,512]{1,0:T(8,128)(2,1)S(1)}, bf16[576,512]{1,0:T(8,128)(2,1)S(1)}, u32[]{:S(2)}, u32[]{:S(2)}) collective-permute-start(bf16[576,512]{1,0:T(8,128)(2,1)S(1)} %add_convert_fusion.1), channel_id=1, source_target_pairs={{4,0},{6,2},{8,4},{10,6},{12,8},{14,10},{16,12},{18,14},{20,16},{2... | collective-permute-start | bytes 1769480 | tf_op jit(solution)/shard_map/ppermute | solution.py:252
  113.9 120.6 %collective-permute-start.7 = (bf16[576,512]{1,0:T(8,128)(2,1)S(1)}, bf16[576,512]{1,0:T(8,128)(2,1)S(1)}, u32[]{:S(2)}, u32[]{:S(2)}) collective-permute-start(bf16[576,512]{1,0:T(8,128)(2,1)S(1)} %fusion), channel_id=1, source_target_pairs={{0,1},{1,0},{2,3},{3,2},{4,5},{5,4},{6,7},{7,6},{8,9},{9,8},{10,11... | collective-permute-start | bytes 1769480 | tf_op jit(solution)/shard_map/ppermute | solution.py:293
Sparse Core Ops, SparseCore 0:
  77.7 89.8 reduce-scatter.2
  171.9 60.9 reduce-scatter.4
where the time goes:
time: 242 us
  waiting for transfers between devices  163 us (67%)
  Pallas kernels  31.4 us (13%)
  starting transfers between devices  25.4 us (10%)
  between operations  14.1 us (6%)
  other arithmetic  7.21 us (3%)
    reduce_scatter x2, waiting for transfers between devices, local(): lax.psum_scatter(both, 'ctx', scatter_dimension=0, axis_index_groups=chip...  117 us
    ppermute x8, waiting for transfers between devices, permute(): return lax.ppermute(value, axis, pairs)  46 us
    pallas_call x2, Pallas kernels, attention(): pl.pallas_call(functools.partial(attention_kernel, rows, ranks, initial,...  31.4 us
    ppermute x8, starting transfers between devices, permute(): return lax.ppermute(value, axis, pairs)  23.8 us
  transfers between devices with their start and end apart: 11, of which 7 were waited for; matrix products, arithmetic and copies ran while one was open for 2% of the time, Pallas kernels for 0%

commit v1 on v0

--- a/solution.py
+++ b/solution.py
@@ -17,7 +17,6 @@
 KV = NOPE + VDIM
 WIDTH = LATENT + ROPE
 TILE = 256
-GROUPS = 2
 
 MASKED = -1e30
 FLOOR = -1e20
@@ -183,14 +182,12 @@
             x_copy.wait()
 
 
-def attention(index, doc_ids, queries, grad_out, weight, blocks, state, group, groups, ranks):
+def attention(index, doc_ids, queries, grad_out, weight, blocks, state, span, total, ranks):
     rows = queries.shape[0]
-    heads = weight.shape[1] // KV
-    pairs = heads // 2 // groups
-    first = group * pairs
+    first, pairs = span[0], span[1] - span[0]
     window = (REACH + 1) * rows
     low, full = jnp.bfloat16, jnp.float32
-    initial, final = group == 0, group == groups - 1
+    initial, final = span[0] == 0, span[1] == total
     anywhere = pl.BlockSpec(memory_space=pl.ANY)
     scalars = pl.BlockSpec(memory_space=pltpu.SMEM)
 
@@ -263,23 +260,26 @@
     swapped = permute(far, "ctx", lambda s: s ^ 1)
     blocks = (swapped, far, mixed, latent)
 
-    groups = min(GROUPS, kv_up_weight.shape[1] // (2 * KV))
+    pairs = kv_up_weight.shape[1] // (2 * KV)
+    spans = [(0, pairs - 1), (pairs - 1, pairs)] if pairs > 1 else [(0, pairs)]
     chips = [list(range(parity, ranks, 2)) for parity in range(2)]
-    state, grad_weight = (), []
-    for group in range(groups):
+    state, arrived = (), []
+    for span in spans:
         grad_queries, keep, send, *parts = attention(
-            index, doc_ids, queries, grad_out, kv_up_weight, blocks, state, group, groups, ranks
+            index, doc_ids, queries, grad_out, kv_up_weight, blocks, state, span, pairs, ranks
         )
+        if arrived:
+            arrived[-1], send, *parts = lax.optimization_barrier((arrived[-1], send, *parts))
         both = keep.astype(full) + permute(send, "ctx", lambda s: s ^ 1).astype(full)
         both = both.astype(low)
-        if group < groups - 1:
+        if span[1] < pairs:
             both, *parts = lax.optimization_barrier((both, *parts))
         state = (grad_queries, *parts)
-        grad_weight.append(
-            lax.psum_scatter(
-                both, "ctx", scatter_dimension=0, axis_index_groups=chips, tiled=True
-            ).astype(full)
-        )
+        arrived.append(lax.all_to_all(both, "ctx", 0, 0, axis_index_groups=chips, tiled=True))
+    grad_weight = [
+        jnp.sum(pieces.reshape(ranks // 2, LATENT // ranks, -1).astype(full), axis=0)
+        for pieces in arrived
+    ]
 
     to_swap, to_far, to_mixed, mine = parts
     from_mixed = permute(to_mixed, "ctx", lambda s: s - 1 if s % 2 else s - 3)

time: 242 us -> 148 us (0.61)
  waiting for transfers between devices: 163 us -> 47.8 us
  starting transfers between devices: 25.4 us -> 58.2 us
  between operations: 14.1 us -> 0.72 us
    reduce_scatter x2 -> x0, waiting for transfers between devices: 117 us -> none  [local(): lax.psum_scatter(both, 'ctx', scatter_dimension=0, axis_index_groups=chip...]
    all_to_all x0 -> x2, starting transfers between devices: none -> 36.5 us  [local(): lax.all_to_all(both, 'ctx', 0, 0, axis_index_groups=chips, tiled=True)]
    ppermute x8, waiting for transfers between devices: 46 us -> 25.9 us  [permute(): return lax.ppermute(value, axis, pairs)]
    all_to_all x0 -> x2, waiting for transfers between devices: none -> 16.1 us  [local(): lax.all_to_all(both, 'ctx', 0, 0, axis_index_groups=chips, tiled=True)]
    ppermute x1, waiting for transfers between devices: 0.01 us -> 5.76 us  [local(): lax.ppermute(mine, 'head', [(s, (s + turn) % size) for s in range(size)])]
    ppermute x8, starting transfers between devices: 23.8 us -> 20.2 us  [permute(): return lax.ppermute(value, axis, pairs)]
  transfers between devices with their start and end apart: 11 -> 11, of which waited for: 7 -> 9; matrix products, arithmetic and copies ran while one was open for 2% -> 3% of each run, Pallas kernels for 0% -> 7%
where the time goes in v1:
time: 148 us; the launch traced here: 147 us
  starting transfers between devices  58.2 us (39%)
  waiting for transfers between devices  47.8 us (32%)
  Pallas kernels  31.1 us (21%)
  other arithmetic  8.28 us (6%)
    all_to_all x2, starting transfers between devices, local(): lax.all_to_all(both, 'ctx', 0, 0, axis_index_groups=chips, tiled=True)  36.5 us
    pallas_call x2, Pallas kernels, attention(): pl.pallas_call(functools.partial(attention_kernel, rows, ranks, initial,...  31.1 us
    ppermute x8, waiting for transfers between devices, permute(): return lax.ppermute(value, axis, pairs)  25.9 us
    ppermute x8, starting transfers between devices, permute(): return lax.ppermute(value, axis, pairs)  20.2 us
    all_to_all x2, waiting for transfers between devices, local(): lax.all_to_all(both, 'ctx', 0, 0, axis_index_groups=chips, tiled=True)  16.1 us
    ppermute x1, waiting for transfers between devices, local(): lax.ppermute(mine, 'head', [(s, (s + turn) % size) for s in range(size)])  5.76 us
    convert_element_type x2, other arithmetic, local(): both = both.astype(low)  2.98 us
  transfers between devices with their start and end apart: 11, of which 9 were waited for; matrix products, arithmetic and copies ran while one was open for 3% of the time, Pallas kernels for 7%

profile of v1, /device:TPU:0, one launch (start us, length us, event | category | flops | bytes accessed | tf_op | source)
XLA Modules:
  0.0 146.9 jit_solution(5180123090942908064)
XLA Ops:
  0.6 4.9 %collective-permute-start = (bf16[576,512]{1,0:T(8,128)(2,1)}, bf16[576,512]{1,0:T(8,128)(2,1)S(1)}, u32[]{:S(2)}, u32[]{:S(2)}) collective-permute-start(bf16[576,512]{1,0:T(8,128)(2,1)} %bitcast.10), channel_id=1, source_target_pairs={{0,4},{2,6},{4,8},{6,10},{8,12},{10,14},{12,16},{14,18},{16,20},{1... | collective-permute-start | bytes 1769480 | tf_op jit(solution)/shard_map/ppermute | solution.py:249
  5.5 1.5 %collective-permute-start.2 = (bf16[576,512]{1,0:T(8,128)(2,1)}, bf16[576,512]{1,0:T(8,128)(2,1)S(1)}, u32[]{:S(2)}, u32[]{:S(2)}) collective-permute-start(bf16[576,512]{1,0:T(8,128)(2,1)} %bitcast.11), channel_id=1, source_target_pairs={{0,2},{2,8},{4,6},{6,12},{8,10},{10,16},{12,14},{14,20},{16,18},{1... | collective-permute-start | bytes 1769480 | tf_op jit(solution)/shard_map/ppermute | solution.py:249
  7.0 11.3 %collective-permute-done.refs_7_ = bf16[576,512]{1,0:T(8,128)(2,1)S(1)} collective-permute-done((bf16[576,512]{1,0:T(8,128)(2,1)}, bf16[576,512]{1,0:T(8,128)(2,1)S(1)}, u32[]{:S(2)}, u32[]{:S(2)}) %collective-permute-start) | collective-permute-done | bytes 589856 | tf_op jit(solution)/shard_map/ppermute | solution.py:249
  18.4 0.0 copy-start.2
  18.4 0.0 collective-permute-start.1
  18.4 0.0 collective-permute-done.2.refs_8_
  18.4 0.0 copy-start.3
  18.4 2.0 %collective-permute-done.1.refs_6_ = bf16[576,512]{1,0:T(8,128)(2,1)S(1)} collective-permute-done((bf16[576,512]{1,0:T(8,128)(2,1)S(1)}, bf16[576,512]{1,0:T(8,128)(2,1)S(1)}, u32[]{:S(2)}, u32[]{:S(2)}) %collective-permute-start.1) | collective-permute-done | bytes 589856 | tf_op jit(solution)/shard_map/ppermute | solution.py:249
  20.4 0.0 copy-start.4
  20.4 0.0 copy-done.2
  20.4 0.0 copy-done.3
  20.4 0.8 copy-done.4
  21.2 20.3 %attention.2 = (bf16[512,1536]{1,0:T(8,128)(2,1)}, bf16[256,1536]{1,0:T(8,128)(2,1)}, bf16[256,1536]{1,0:T(8,128)(2,1)}, f32[576,2048]{1,0:T(8,128)}) custom-call(s32[1]{0:T(128)} %bitcast.refs_0_, s32[8192]{0:T(1024)} %refs_1_.3, s32[1,8192]{1,0:T(1,128)} %bitcast.14, bf16[512,1536]{1,0:T(8,128)(2,1)} %refs_3_.3, bf16[512,1024]{1,0:T(8,128)(2,1)} %refs_4_.3, ...), custom_call_target="tpu_custom_call" | custom-call | flops 20937965568 | bytes 16777216 | tf_op jit(solution)/shard_map/attention/pallas_call | solution.py:200
  41.5 10.7 %collective-permute-start.3 = (bf16[256,1536]{1,0:T(8,128)(2,1)}, bf16[256,1536]{1,0:T(8,128)(2,1)S(1)}, u32[]{:S(2)}, u32[]{:S(2)}) collective-permute-start(bf16[256,1536]{1,0:T(8,128)(2,1)} %get-tuple-element.24), channel_id=1, source_target_pairs={{0,2},{2,0},{4,6},{6,4},{8,10},{10,8},{12,14},{14,12},{16,18},{18,... | collective-permute-start | bytes 2359304 | tf_op jit(solution)/shard_map/ppermute | solution.py:249
  52.2 2.1 %collective-permute-done.3 = bf16[256,1536]{1,0:T(8,128)(2,1)S(1)} collective-permute-done((bf16[256,1536]{1,0:T(8,128)(2,1)}, bf16[256,1536]{1,0:T(8,128)(2,1)S(1)}, u32[]{:S(2)}, u32[]{:S(2)}) %collective-permute-start.3) | collective-permute-done | bytes 786464 | tf_op jit(solution)/shard_map/ppermute | solution.py:249
  54.3 2.2 %add_convert_fusion = bf16[256,1536]{1,0:T(8,128)(2,1)} fusion(bf16[256,1536]{1,0:T(8,128)(2,1)S(1)} %collective-permute-done.3, bf16[256,1536]{1,0:T(8,128)(2,1)} %get-tuple-element.23), kind=kLoop, calls=%fused_computation.1 | loop fusion | flops 1572864 | bytes 2359296 | tf_op jit(solution)/shard_map/convert_element_type | solution.py:274
  56.5 29.1 %all-to-all-start = ((bf16[8,32,1536]{2,1,0:T(8,128)(2,1)}), bf16[8,32,1536]{2,1,0:T(8,128)(2,1)S(1)}, u32[]{:S(2)}, u32[]{:S(2)}) async-start(bf16[8,32,1536]{2,1,0:T(8,128)(2,1)} %bitcast.3), calls=%async_computation | async-start | bytes 1572864 | tf_op jit(solution)/shard_map/all_to_all | solution.py:278
  85.7 10.8 %attention.3 = (bf16[512,1536]{1,0:T(8,128)(2,1)}, bf16[256,512]{1,0:T(8,128)(2,1)}, bf16[256,512]{1,0:T(8,128)(2,1)}, bf16[576,512]{1,0:T(8,128)(2,1)}, bf16[57...) custom-call(s32[1]{0:T(128)} %bitcast.refs_0_, ...), custom_call_target="tpu_custom_call", output_to_operand_aliasing={{0}: (10, {})} | custom-call | flops 6979321856 | bytes 16777216 | tf_op jit(solution)/shard_map/attention/pallas_call | solution.py:200
  96.4 0.0 copy-start.1
  96.5 9.9 %all-to-all-done = bf16[8,32,1536]{2,1,0:T(8,128)(2,1)S(1)} async-done(((bf16[8,32,1536]{2,1,0:T(8,128)(2,1)}), bf16[8,32,1536]{2,1,0:T(8,128)(2,1)S(1)}, u32[]{:S(2)}, u32[]{:S(2)}) %all-to-all-start) | async-done | bytes 786464 | tf_op jit(solution)/shard_map/all_to_all | solution.py:278
  106.3 0.0 copy-start.5
  106.3 0.0 copy-start
  106.3 0.0 collective-permute-start.5
  106.4 1.4 collective-permute-start.4
  107.8 0.8 collective-permute-done.5
  108.6 1.2 add_convert_fusion.2
  109.8 1.3 collective-permute-start.6
  111.1 0.0 copy-done.5
  111.1 0.4 collective-permute-start.8
  111.5 1.2 collective-permute-done.8
  112.7 0.0 copy-done.1
  112.7 0.8 add_convert_fusion.3
  113.5 7.4 %all-to-all-start.1 = ((bf16[8,32,512]{2,1,0:T(8,128)(2,1)}), bf16[8,32,512]{2,1,0:T(8,128)(2,1)S(1)}, u32[]{:S(2)}, u32[]{:S(2)}) async-start(bf16[8,32,512]{2,1,0:T(8,128)(2,1)} %bitcast.7), calls=%async_computation.1 | async-start | bytes 524288 | tf_op jit(solution)/shard_map/all_to_all | solution.py:278
  120.9 0.0 collective-permute-done.4
  120.9 8.5 %collective-permute-done.6 = bf16[576,512]{1,0:T(8,128)(2,1)S(1)} collective-permute-done((bf16[576,512]{1,0:T(8,128)(2,1)S(1)}, bf16[576,512]{1,0:T(8,128)(2,1)S(1)}, u32[]{:S(2)}, u32[]{:S(2)}) %collective-permute-start.6) | collective-permute-done | bytes 589856 | tf_op jit(solution)/shard_map/ppermute | solution.py:249
  129.4 0.0 copy-done
  129.4 1.0 fusion
  130.4 1.5 collective-permute-start.7
  131.9 0.1 convert_reduce_fusion
  132.0 6.2 %all-to-all-done.1 = bf16[8,32,512]{2,1,0:T(8,128)(2,1)S(1)} async-done(((bf16[8,32,512]{2,1,0:T(8,128)(2,1)}), bf16[8,32,512]{2,1,0:T(8,128)(2,1)S(1)}, u32[]{:S(2)}, u32[]{:S(2)}) %all-to-all-start.1) | async-done | bytes 262176 | tf_op jit(solution)/shard_map/all_to_all | solution.py:278
  138.3 0.7 pad_maximum_fusion
  139.0 5.8 %collective-permute-done.7 = bf16[576,512]{1,0:T(8,128)(2,1)} collective-permute-done((bf16[576,512]{1,0:T(8,128)(2,1)}, bf16[576,512]{1,0:T(8,128)(2,1)}, u32[]{:S(2)}, u32[]{:S(2)}) %collective-permute-start.7) | collective-permute-done | bytes 589856 | tf_op jit(solution)/shard_map/ppermute | solution.py:293
  144.7 2.2 %fusion.1 = bf16[512,576]{0,1:T(8,128)(2,1)} fusion(bf16[576,512]{1,0:T(8,128)(2,1)} %collective-permute-done.7, bf16[576,512]{1,0:T(8,128)(2,1)S(1)} %collective-permute-done.6, bf16[576,512]{1,0:T(8,128)(2,1)S(1)} %collective-permute-done.4, bf16[576,512]{1,0:T(8,128)(2,1)S(1)} %copy-done), kind=kLoop, calls=%fused_computation.6 | loop fusion | flops 2359296 | bytes 2949120 | tf_op jit(solution)/shard_map/transpose | solution.py:295
  (1 shorter events, 0.0 us)
Async XLA Ops:
  0.6 17.7 %collective-permute-start = (bf16[576,512]{1,0:T(8,128)(2,1)}, bf16[576,512]{1,0:T(8,128)(2,1)S(1)}, u32[]{:S(2)}, u32[]{:S(2)}) collective-permute-start(bf16[576,512]{1,0:T(8,128)(2,1)} %bitcast.10), channel_id=1, source_target_pairs={{0,4},{2,6},{4,8},{6,10},{8,12},{10,14},{12,16},{14,18},{16,20},{1... | collective-permute-start | bytes 1769480 | tf_op jit(solution)/shard_map/ppermute | solution.py:249
  5.5 12.9 %collective-permute-start.2 = (bf16[576,512]{1,0:T(8,128)(2,1)}, bf16[576,512]{1,0:T(8,128)(2,1)S(1)}, u32[]{:S(2)}, u32[]{:S(2)}) collective-permute-start(bf16[576,512]{1,0:T(8,128)(2,1)} %bitcast.11), channel_id=1, source_target_pairs={{0,2},{2,8},{4,6},{6,12},{8,10},{10,16},{12,14},{14,20},{16,18},{1... | collective-permute-start | bytes 1769480 | tf_op jit(solution)/shard_map/ppermute | solution.py:249
  18.4 2.0 %copy-start.2 = (bf16[576,512]{1,0:T(8,128)(2,1)}, bf16[576,512]{1,0:T(8,128)(2,1)S(1)}, u32[]{:S(2)}) copy-start(bf16[576,512]{1,0:T(8,128)(2,1)S(1)} %collective-permute-done.refs_7_) | copy-start | bytes 1769476
  18.4 2.0 %collective-permute-start.1 = (bf16[576,512]{1,0:T(8,128)(2,1)S(1)}, bf16[576,512]{1,0:T(8,128)(2,1)S(1)}, u32[]{:S(2)}, u32[]{:S(2)}) collective-permute-start(bf16[576,512]{1,0:T(8,128)(2,1)S(1)} %collective-permute-done.refs_7_), channel_id=1, source_target_pairs={{0,2},{2,0},{4,6},{6,4},{8,10},{10,8},{12,14},{14,12},{16,18},{18,... | collective-permute-start | bytes 1769480 | tf_op jit(solution)/shard_map/ppermute | solution.py:249
  18.4 2.0 %copy-start.3 = (bf16[576,512]{1,0:T(8,128)(2,1)}, bf16[576,512]{1,0:T(8,128)(2,1)S(1)}, u32[]{:S(2)}) copy-start(bf16[576,512]{1,0:T(8,128)(2,1)S(1)} %collective-permute-done.2.refs_8_) | copy-start | bytes 1769476
  20.4 0.8 copy-start.4
  41.5 12.8 %collective-permute-start.3 = (bf16[256,1536]{1,0:T(8,128)(2,1)}, bf16[256,1536]{1,0:T(8,128)(2,1)S(1)}, u32[]{:S(2)}, u32[]{:S(2)}) collective-permute-start(bf16[256,1536]{1,0:T(8,128)(2,1)} %get-tuple-element.24), channel_id=1, source_target_pairs={{0,2},{2,0},{4,6},{6,4},{8,10},{10,8},{12,14},{14,12},{16,18},{18,... | collective-permute-start | bytes 2359304 | tf_op jit(solution)/shard_map/ppermute | solution.py:249
  56.5 49.8 %all-to-all-start = ((bf16[8,32,1536]{2,1,0:T(8,128)(2,1)}), bf16[8,32,1536]{2,1,0:T(8,128)(2,1)S(1)}, u32[]{:S(2)}, u32[]{:S(2)}) async-start(bf16[8,32,1536]{2,1,0:T(8,128)(2,1)} %bitcast.3), calls=%async_computation | async-start | bytes 1572864 | tf_op jit(solution)/shard_map/all_to_all | solution.py:278
  96.4 16.3 %copy-start.1 = (bf16[256,512]{1,0:T(8,128)(2,1)S(1)}, bf16[256,512]{1,0:T(8,128)(2,1)}, u32[]{:S(2)}) copy-start(bf16[256,512]{1,0:T(8,128)(2,1)} %get-tuple-element.39) | copy-start | bytes 786436
  106.3 4.7 %copy-start.5 = (bf16[256,512]{1,0:T(8,128)(2,1)S(1)}, bf16[256,512]{1,0:T(8,128)(2,1)}, u32[]{:S(2)}) copy-start(bf16[256,512]{1,0:T(8,128)(2,1)} %get-tuple-element.40) | copy-start | bytes 786436
  106.3 23.0 %copy-start = (bf16[576,512]{1,0:T(8,128)(2,1)S(1)}, bf16[576,512]{1,0:T(8,128)(2,1)}, u32[]{:S(2)}) copy-start(bf16[576,512]{1,0:T(8,128)(2,1)} %get-tuple-element.34) | copy-start | bytes 1769476
  106.3 2.2 %collective-permute-start.5 = (bf16[576,512]{1,0:T(8,128)(2,1)}, bf16[576,512]{1,0:T(8,128)(2,1)S(1)}, u32[]{:S(2)}, u32[]{:S(2)}) collective-permute-start(bf16[576,512]{1,0:T(8,128)(2,1)} %get-tuple-element.37), channel_id=1, source_target_pairs={{0,2},{2,0},{4,6},{6,4},{8,10},{10,8},{12,14},{14,12},{16,18},{18,... | collective-permute-start | bytes 1769480 | tf_op jit(solution)/shard_map/ppermute | solution.py:249
  106.4 14.5 %collective-permute-start.4 = (bf16[576,512]{1,0:T(8,128)(2,1)}, bf16[576,512]{1,0:T(8,128)(2,1)S(1)}, u32[]{:S(2)}, u32[]{:S(2)}) collective-permute-start(bf16[576,512]{1,0:T(8,128)(2,1)} %get-tuple-element.35), channel_id=1, source_target_pairs={{2,0},{6,4},{8,2},{10,8},{12,6},{14,12},{16,10},{18,16},{20,14},{2... | collective-permute-start | bytes 1769480 | tf_op jit(solution)/shard_map/ppermute | solution.py:249
  109.8 19.6 %collective-permute-start.6 = (bf16[576,512]{1,0:T(8,128)(2,1)S(1)}, bf16[576,512]{1,0:T(8,128)(2,1)S(1)}, u32[]{:S(2)}, u32[]{:S(2)}) collective-permute-start(bf16[576,512]{1,0:T(8,128)(2,1)S(1)} %add_convert_fusion.2), channel_id=1, source_target_pairs={{4,0},{6,2},{8,4},{10,6},{12,8},{14,10},{16,12},{18,14},{20,16},{2... | collective-permute-start | bytes 1769480 | tf_op jit(solution)/shard_map/ppermute | solution.py:249
  111.1 1.6 %collective-permute-start.8 = (bf16[256,512]{1,0:T(8,128)(2,1)S(1)}, bf16[256,512]{1,0:T(8,128)(2,1)S(1)}, u32[]{:S(2)}, u32[]{:S(2)}) collective-permute-start(bf16[256,512]{1,0:T(8,128)(2,1)S(1)} %copy-done.5), channel_id=1, source_target_pairs={{0,2},{2,0},{4,6},{6,4},{8,10},{10,8},{12,14},{14,12},{16,18},{18,... | collective-permute-start | bytes 786440 | tf_op jit(solution)/shard_map/ppermute | solution.py:249
  113.5 24.7 %all-to-all-start.1 = ((bf16[8,32,512]{2,1,0:T(8,128)(2,1)}), bf16[8,32,512]{2,1,0:T(8,128)(2,1)S(1)}, u32[]{:S(2)}, u32[]{:S(2)}) async-start(bf16[8,32,512]{2,1,0:T(8,128)(2,1)} %bitcast.7), calls=%async_computation.1 | async-start | bytes 524288 | tf_op jit(solution)/shard_map/all_to_all | solution.py:278
  130.4 14.3 %collective-permute-start.7 = (bf16[576,512]{1,0:T(8,128)(2,1)}, bf16[576,512]{1,0:T(8,128)(2,1)}, u32[]{:S(2)}, u32[]{:S(2)}) collective-permute-start(bf16[576,512]{1,0:T(8,128)(2,1)} %fusion), channel_id=1, source_target_pairs={{0,1},{1,0},{2,3},{3,2},{4,5},{5,4},{6,7},{7,6},{8,9},{9,8},{10,11... | collective-permute-start | bytes 1769480 | tf_op jit(solution)/shard_map/ppermute | solution.py:293

commit v2 on v1

v2 whole, which is shorter than its diff:
```python
import functools
import math

import jax
import jax.numpy as jnp
from jax import lax
from jax.experimental import pallas as pl
from jax.experimental.pallas import tpu as pltpu
from jax.sharding import PartitionSpec as P

NOPE = 128
ROPE = 64
VDIM = 128
LATENT = 512
REACH = 3
QK = NOPE + ROPE
KV = NOPE + VDIM
WIDTH = LATENT + ROPE
LANES = 128

MASKED = -1e30
FLOOR = -1e20
SCALE = 1.0 / math.sqrt(QK)
SCALE2 = SCALE * math.log2(math.e)

NT = (((1,), (1,)), ((), ()))
NN = (((1,), (0,)), ((), ()))


def dot(a, b, dims=NN):
    return lax.dot_general(a, b, dims, preferred_element_type=jnp.float32)


def attention_kernel(rows, ranks, *refs):
    (index_ref, docs_sref, docs_ref, qa_ref, doa_ref, wa_ref, qc_ref, doc_ref, wc_ref,
     lat0, lat1, lat2, lat3, dq_ref, keep_ref, send_ref, x0_ref, x1_ref, x2_ref, x3_ref,
     lat_ref, lat_t_ref, bias_ref, e_ref, g_ref, k_ref, top_ref, run_ref, end_ref,
     dq_acc, gw_acc, x_acc, r_acc, sems) = refs

    step, last = pl.program_id(0), pl.num_programs(0) - 1
    index = index_ref[0]
    odd = lax.rem(index, 2)
    first_row = index * rows
    first_doc = docs_sref[first_row]
    heads = range(2)

    def window_base(t):
        base = jnp.where(t == 1, rows, REACH * rows)
        base = jnp.where(t == 0, rows * 2 * (1 - odd), base)
        return jnp.where(t == 2, rows * 2 * odd, base)

    def active(t):
        position = first_row - REACH * rows + window_base(t)
        last_doc = docs_sref[jnp.maximum(position, 0) + rows - 1]
        return (position >= 0) & (last_doc >= first_doc)

    def block_rows(t):
        return pl.ds(pl.multiple_of(t * rows, rows), rows)

    def each_block(body):
        def visit(t, carry):
            @pl.when(active(t))
            def _():
                body(t)

            return carry

        lax.fori_loop(0, REACH + 1, visit, 0)

    def fill_bias(t):
        base = window_base(t)
        my_docs = docs_ref[:, pl.ds(pl.multiple_of(first_row, rows), rows)]
        last_seen = REACH * rows + lax.broadcasted_iota(jnp.int32, (1, rows), 1)
        position = pl.multiple_of(first_row - REACH * rows + base, rows)
        key_docs = docs_ref[:, pl.ds(position, rows)]
        key_docs = jnp.broadcast_to(key_docs, (128, rows)).T[:, :1]
        key = lax.broadcasted_iota(jnp.int32, (rows, rows), 0)
        seen = (key_docs == my_docs) & (key <= last_seen - base)
        bias_ref[block_rows(t), :] = jnp.where(seen, 0.0, MASKED)

    @pl.when(step == 0)
    def _():
        copies = [
            pltpu.make_async_copy(source, lat_t_ref.at[:, pl.ds(i * rows, rows)], sems.at[i])
            for i, source in enumerate((lat0, lat1, lat2, lat3))
        ]
        for copy in copies:
            copy.start()
        x_acc[...] = jnp.zeros_like(x_acc)
        r_acc[...] = jnp.zeros_like(r_acc)
        each_block(fill_bias)
        for copy in copies:
            copy.wait()
        for i in range(REACH + 1):
            part = slice(i * rows, (i + 1) * rows)
            lat_ref[part, :] = lat_t_ref[:, part].T

    def take_probs(t):
        part = block_rows(t)
        out = []
        for h in heads:
            factor = jnp.exp2(top_ref[h, t, 0:1, :] - end_ref[h, 0:1, :]) * end_ref[h, 1:2, :]
            delta = end_ref[h, 2:3, :]
            lows, dscores = [], []
            for c in range(0, rows, LANES):
                cols = slice(c, c + LANES)
                probs = e_ref[h, part, cols] * factor[:, cols]
                dscore = probs * (g_ref[h, part, cols] - delta[:, cols])
                lows.append(probs.astype(jnp.bfloat16))
                dscores.append(dscore.astype(jnp.bfloat16))
            out.append(
                (
                    jnp.concatenate(lows, axis=1),
                    jnp.concatenate(dscores, axis=1),
                    k_ref[h, part, :].T,
                )
            )
        return out

    def add_grads(t, taken):
        part = block_rows(t)
        pieces = []
        for h in heads:
            low, dscore, key_t = taken[h]
            dvalue = dot(low, doc_ref[:, h * VDIM : (h + 1) * VDIM])
            dkey = dot(dscore, qc_ref[:, h * QK : (h + 1) * QK]) * SCALE
            dq_acc[h * QK : (h + 1) * QK, :] += dot(key_t, dscore)
            r_acc[part, :] += dkey[:, NOPE:]
            pieces += [dkey[:, :NOPE].astype(jnp.bfloat16), dvalue.astype(jnp.bfloat16)]
        grads = jnp.concatenate(pieces, axis=1)
        x_acc[:LATENT, part] += dot(wc_ref[...], grads, NT)
        gw_acc[...] += dot(lat_t_ref[:LATENT, part], grads)

    def make_scores(t):
        part = block_rows(t)
        latent = lat_ref[part, :LATENT]
        rope = lat_ref[part, LATENT:]
        out = []
        for h in heads:
            lifted = dot(latent, wa_ref[:, h * KV : (h + 1) * KV]).astype(jnp.bfloat16)
            key = jnp.concatenate([lifted[:, :NOPE], rope], axis=1)
            raw = dot(key, qa_ref[:, h * QK : (h + 1) * QK], NT)
            grads = dot(lifted[:, NOPE:], doa_ref[:, h * VDIM : (h + 1) * VDIM], NT)
            out.append((key, raw, grads))
        return out

    def keep_scores(t, made):
        part = block_rows(t)
        for h in heads:
            key, raw, grads = made[h]
            k_ref[h, part, :] = key
            g_ref[h, part, :] = grads
            for c in range(0, rows, LANES):
                cols = slice(c, c + LANES)
                scores = raw[:, cols] * SCALE2 + bias_ref[part, cols]
                old_top = run_ref[h, 0:1, cols]
                new_top = jnp.maximum(old_top, jnp.max(scores, axis=0, keepdims=True))
                weights = jnp.exp2(scores - new_top)
                e_ref[h, part, cols] = weights
                factor = jnp.exp2(old_top - new_top)
                run_ref[h, 0:1, cols] = new_top
                run_ref[h, 1:2, cols] = run_ref[h, 1:2, cols] * factor + jnp.sum(
                    weights, axis=0, keepdims=True
                )
                run_ref[h, 2:3, cols] = run_ref[h, 2:3, cols] * factor + jnp.sum(
                    weights * grads[:, cols], axis=0, keepdims=True
                )
                top_ref[h, t, 0:1, cols] = new_top

    @pl.when(step > 0)
    def _():
        for h in heads:
            inverse = 1.0 / run_ref[h, 1:2, :]
            end_ref[h, 0:1, :] = run_ref[h, 0:1, :]
            end_ref[h, 1:2, :] = inverse
            end_ref[h, 2:3, :] = run_ref[h, 2:3, :] * inverse
        gw_acc[...] = jnp.zeros_like(gw_acc)
        dq_acc[...] = jnp.zeros_like(dq_acc)

    for h in heads:
        run_ref[h, 0:1, :] = jnp.full((1, rows), FLOOR, jnp.float32)
        run_ref[h, 1:3, :] = jnp.zeros((2, rows), jnp.float32)

    @pl.when(step == 0)
    def _():
        each_block(lambda t: keep_scores(t, make_scores(t)))

    @pl.when((step > 0) & (step < last))
    def _():
        def both(t):
            taken = take_probs(t)
            made = make_scores(t)
            add_grads(t, taken)
            keep_scores(t, made)

        each_block(both)

    @pl.when(step == last)
    def _():
        each_block(lambda t: add_grads(t, take_probs(t)))

    @pl.when(step > 0)
    def _():
        dq_ref[...] = (dq_acc[...] * SCALE).T.astype(dq_ref.dtype)
        share = LATENT // ranks
        quarter = LATENT // 4
        own_x = lax.rem(index // 2, 2)
        for i in range(ranks // 4):
            for out, core in ((keep_ref, odd), (send_ref, 1 - odd)):
                for where, x in ((0, own_x), (quarter, 1 - own_x)):
                    source = pl.multiple_of((4 * i + 2 * x + core) * share, share)
                    out[where + i * share : where + (i + 1) * share, :] = gw_acc[
                        pl.ds(source, share), :
                    ].astype(out.dtype)

    @pl.when(step == last)
    def _():
        x_acc[LATENT:, :] = r_acc[...].T
        for i, out in enumerate((x0_ref, x1_ref, x2_ref, x3_ref)):
            out[...] = x_acc[:, i * rows : (i + 1) * rows].astype(out.dtype)


def attention(index, doc_ids, queries, grad_out, weight, blocks, ranks):
    rows = queries.shape[0]
    pairs = weight.shape[1] // (2 * KV)
    window = (REACH + 1) * rows
    low, full = jnp.bfloat16, jnp.float32
    scalars = pl.BlockSpec(memory_space=pltpu.SMEM)

    def pair_cols(height, size, pair):
        return pl.BlockSpec((height, 2 * size), lambda i: (0, pair(i)))

    def inputs(pair):
        return [
            pair_cols(rows, QK, pair), pair_cols(rows, VDIM, pair), pair_cols(LATENT, KV, pair)
        ]

    def ahead(i):
        return jnp.minimum(i, pairs - 1)

    def behind(i):
        return jnp.maximum(i - 1, 0)

    half = pair_cols(LATENT // 2, KV, behind)
    half_shape = jax.ShapeDtypeStruct((LATENT // 2, pairs * 2 * KV), low)
    flops = 2 * pairs * 2 * rows * window * (3 * QK + 2 * VDIM) * 2
    return pl.pallas_call(
        functools.partial(attention_kernel, rows, ranks),
        grid=(pairs + 1,),
        in_specs=[scalars, scalars, pl.BlockSpec((1, doc_ids.shape[0]), lambda i: (0, 0))]
        + inputs(ahead)
        + inputs(behind)
        + [pl.BlockSpec(memory_space=pl.ANY)] * (REACH + 1),
        out_specs=[pair_cols(rows, QK, behind), half, half]
        + [pl.BlockSpec((WIDTH, rows), lambda i: (0, 0))] * (REACH + 1),
        out_shape=[jax.ShapeDtypeStruct(queries.shape, low), half_shape, half_shape]
        + [jax.ShapeDtypeStruct((WIDTH, rows), low)] * (REACH + 1),
        scratch_shapes=[
            pltpu.VMEM((window, WIDTH), low),
            pltpu.VMEM((WIDTH, window), low),
            pltpu.VMEM((window, rows), full),
            pltpu.VMEM((2, window, rows), full),
            pltpu.VMEM((2, window, rows), full),
            pltpu.VMEM((2, window, QK), low),
            pltpu.VMEM((2, REACH + 1, 8, rows), full),
            pltpu.VMEM((2, 8, rows), full),
            pltpu.VMEM((2, 8, rows), full),
            pltpu.VMEM((2 * QK, rows), full),
            pltpu.VMEM((LATENT, 2 * KV), full),
            pltpu.VMEM((WIDTH, window), full),
            pltpu.VMEM((window, ROPE), full),
            pltpu.SemaphoreType.DMA((REACH + 1,)),
        ],
        compiler_params=pltpu.CompilerParams(
            dimension_semantics=("arbitrary",), vmem_limit_bytes=56 * 1024 * 1024
        ),
        cost_estimate=pl.CostEstimate(
            flops=flops, bytes_accessed=16 * 1024 * 1024, transcendentals=0
        ),
        name="attention",
    )(index, doc_ids, doc_ids[None], *(queries, grad_out, weight) * 2, *blocks)


def permute(value, axis, target):
    count = lax.axis_size(axis)
    pairs = [(s, target(s)) for s in range(count) if 0 <= target(s) < count]
    return lax.ppermute(value, axis, pairs)


def local(kv_latent, queries, grad_out, kv_up_weight, doc_ids):
    ranks = lax.axis_size("ctx")
    index = lax.axis_index("ctx").astype(jnp.int32)[None]
    low, full = jnp.bfloat16, jnp.float32

    latent = kv_latent.T
    far = permute(latent, "ctx", lambda s: s + 2)
    mixed = permute(latent, "ctx", lambda s: s + 3 if s % 2 else s + 1)
    swapped = permute(far, "ctx", lambda s: s ^ 1)
    blocks = (swapped, far, mixed, latent)

    grad_queries, keep, send, to_swap, to_far, to_mixed, mine = attention(
        index, doc_ids, queries, grad_out, kv_up_weight, blocks, ranks
    )

    chip = keep.astype(full) + permute(send, "ctx", lambda s: s ^ 1).astype(full)
    quarter = LATENT // 4
    from_x = permute(chip[quarter:].astype(low), "ctx", lambda s: s ^ 2)
    plane = (chip[:quarter] + from_x.astype(full)).astype(low)
    columns = [list(range(first, ranks, 4)) for first in range(4)]
    pieces = lax.all_to_all(plane, "ctx", 0, 0, axis_index_groups=columns, tiled=True)
    grad_weight = jnp.sum(pieces.reshape(ranks // 4, LATENT // ranks, -1).astype(full), axis=0)

    from_mixed = permute(to_mixed, "ctx", lambda s: s - 1 if s % 2 else s - 3)
    from_swap = permute(to_swap, "ctx", lambda s: s ^ 1)
    far_sum = (to_far.astype(full) + from_swap.astype(full)).astype(low)
    from_far = permute(far_sum, "ctx", lambda s: s - 2)
    total = mine.astype(full) + from_mixed.astype(full) + from_far.astype(full)
    mine = total.astype(low)
    size = lax.axis_size("head")
    for turn in range(1, size):
        other = lax.ppermute(mine, "head", [(s, (s + turn) % size) for s in range(size)])
        total = total + other.astype(full)
    return grad_queries, total.astype(low).T, grad_weight


def solution(mesh):
    return jax.shard_map(
        local,
        mesh=mesh,
        in_specs=(P("ctx", None), P("ctx", "head"), P("ctx", "head"), P(None, "head"), P()),
        out_specs=(P("ctx", "head"), P("ctx", None), P("ctx", "head")),
        check_vma=False,
    )
```

time: 148 us -> 135 us (0.912)
  Pallas kernels: 31.1 us -> 20.6 us
  other arithmetic: 8.28 us -> 4.6 us
  waiting for transfers between devices: 47.8 us -> 51.1 us
  starting transfers between devices: 58.2 us -> 56.7 us
    all_to_all x2 -> x1, starting transfers between devices: 36.5 us -> 18.2 us  [local(): lax.all_to_all(plane, 'ctx', 0, 0, axis_index_groups=columns, tiled=True)]
    ppermute x8, starting transfers between devices: 20.2 us -> 36.9 us  [permute(): return lax.ppermute(value, axis, pairs)]
    ppermute x8, waiting for transfers between devices: 25.9 us -> 37.8 us  [permute(): return lax.ppermute(value, axis, pairs)]
    pallas_call x2 -> x1, Pallas kernels: 31.1 us -> 20.6 us  [attention(): pl.pallas_call(functools.partial(attention_kernel, rows, ranks), grid=(pa...]
    ppermute x1, waiting for transfers between devices: 5.76 us -> 0.01 us  [local(): lax.ppermute(mine, 'head', [(s, (s + turn) % size) for s in range(size)])]
    all_to_all x2 -> x1, waiting for transfers between devices: 16.1 us -> 13.3 us  [local(): lax.all_to_all(plane, 'ctx', 0, 0, axis_index_groups=columns, tiled=True)]
    convert_element_type x2 -> x1, other arithmetic: 2.98 us -> 0.9 us  [local(): plane = (chip[:quarter] + from_x.astype(full)).astype(low)]
  transfers between devices with their start and end apart: 11 -> 10, of which waited for: 9 -> 6; matrix products, arithmetic and copies ran while one was open for 3% -> 3% of each run, Pallas kernels for 7% -> 0%
where the time goes in v2:
time: 135 us
  starting transfers between devices  56.7 us (42%)
  waiting for transfers between devices  51.1 us (38%)
  Pallas kernels  20.6 us (15%)
  other arithmetic  4.6 us (3%)
    ppermute x8, waiting for transfers between devices, permute(): return lax.ppermute(value, axis, pairs)  37.8 us
    ppermute x8, starting transfers between devices, permute(): return lax.ppermute(value, axis, pairs)  36.9 us
    pallas_call x1, Pallas kernels, attention(): pl.pallas_call(functools.partial(attention_kernel, rows, ranks), grid=(pa...  20.6 us
    all_to_all x1, starting transfers between devices, local(): lax.all_to_all(plane, 'ctx', 0, 0, axis_index_groups=columns, tiled=True)  18.2 us
    all_to_all x1, waiting for transfers between devices, local(): lax.all_to_all(plane, 'ctx', 0, 0, axis_index_groups=columns, tiled=True)  13.3 us
  transfers between devices with their start and end apart: 10, of which 6 were waited for; matrix products, arithmetic and copies ran while one was open for 3% of the time, Pallas kernels for 0%

profile of v2, /device:TPU:0, one launch (start us, length us, event | category | flops | bytes accessed | tf_op | source)
XLA Modules:
  0.0 134.7 jit_solution(4672412452629673076)
XLA Ops:
  0.6 4.9 %collective-permute-start = (bf16[576,512]{1,0:T(8,128)(2,1)}, bf16[576,512]{1,0:T(8,128)(2,1)S(1)}, u32[]{:S(2)}, u32[]{:S(2)}) collective-permute-start(bf16[576,512]{1,0:T(8,128)(2,1)} %bitcast.6), channel_id=1, source_target_pairs={{0,4},{2,6},{4,8},{6,10},{8,12},{10,14},{12,16},{14,18},{16,20},{1... | collective-permute-start | bytes 1769480 | tf_op jit(solution)/shard_map/ppermute | solution.py:287
  5.5 1.5 %collective-permute-start.2 = (bf16[576,512]{1,0:T(8,128)(2,1)}, bf16[576,512]{1,0:T(8,128)(2,1)S(1)}, u32[]{:S(2)}, u32[]{:S(2)}) collective-permute-start(bf16[576,512]{1,0:T(8,128)(2,1)} %bitcast.7), channel_id=1, source_target_pairs={{0,2},{2,8},{4,6},{6,12},{8,10},{10,16},{12,14},{14,20},{16,18},{1... | collective-permute-start | bytes 1769480 | tf_op jit(solution)/shard_map/ppermute | solution.py:287
  7.0 11.3 %collective-permute-done.refs_10_ = bf16[576,512]{1,0:T(8,128)(2,1)S(1)} collective-permute-done((bf16[576,512]{1,0:T(8,128)(2,1)}, bf16[576,512]{1,0:T(8,128)(2,1)S(1)}, u32[]{:S(2)}, u32[]{:S(2)}) %collective-permute-start) | collective-permute-done | bytes 589856 | tf_op jit(solution)/shard_map/ppermute | solution.py:287
  18.4 0.0 copy-start.2
  18.4 0.0 collective-permute-start.1
  18.4 0.0 collective-permute-done.2.refs_11_
  18.4 0.0 copy-start.3
  18.4 2.0 %collective-permute-done.1.refs_9_ = bf16[576,512]{1,0:T(8,128)(2,1)S(1)} collective-permute-done((bf16[576,512]{1,0:T(8,128)(2,1)S(1)}, bf16[576,512]{1,0:T(8,128)(2,1)S(1)}, u32[]{:S(2)}, u32[]{:S(2)}) %collective-permute-start.1) | collective-permute-done | bytes 589856 | tf_op jit(solution)/shard_map/ppermute | solution.py:287
  20.4 0.0 copy-start.4
  20.4 0.0 copy-done.2
  20.4 0.0 copy-done.3
  20.4 0.8 copy-done.4
  21.2 20.6 %attention.1 = (bf16[512,1536]{1,0:T(8,128)(2,1)}, bf16[256,2048]{1,0:T(8,128)(2,1)}, bf16[256,2048]{1,0:T(8,128)(2,1)}, bf16[576,512]{1,0:T(8,128)(2,1)}, bf16[...) custom-call(s32[1]{0:T(128)} %bitcast.refs_0_, s32[8192]{0:T(1024)} %refs_1_.1, ...), custom_call_target="tpu_custom_call" | custom-call | flops 27917287424 | bytes 16777216 | tf_op jit(solution)/shard_map/attention/pallas_call | solution.py:247
  41.8 0.0 copy-start.1
  41.8 12.2 %collective-permute-start.7 = (bf16[256,2048]{1,0:T(8,128)(2,1)}, bf16[256,2048]{1,0:T(8,128)(2,1)S(1)}, u32[]{:S(2)}, u32[]{:S(2)}) collective-permute-start(bf16[256,2048]{1,0:T(8,128)(2,1)} %get-tuple-element.16), channel_id=1, source_target_pairs={{0,2},{2,0},{4,6},{6,4},{8,10},{10,8},{12,14},{14,12},{16,18},{18,... | collective-permute-start | bytes 3145736 | tf_op jit(solution)/shard_map/ppermute | solution.py:287
  54.0 0.1 collective-permute-start.4
  54.1 1.3 collective-permute-start.3
  55.4 2.0 %collective-permute-done.4 = bf16[576,512]{1,0:T(8,128)(2,1)S(1)} collective-permute-done((bf16[576,512]{1,0:T(8,128)(2,1)}, bf16[576,512]{1,0:T(8,128)(2,1)S(1)}, u32[]{:S(2)}, u32[]{:S(2)}) %collective-permute-start.4) | collective-permute-done | bytes 589856 | tf_op jit(solution)/shard_map/ppermute | solution.py:287
  57.4 1.2 add_convert_fusion.1
  58.6 1.3 collective-permute-start.5
  59.9 0.0 collective-permute-done.7
  59.9 0.0 copy-done.1
  59.9 0.4 convert_add_fusion
  60.3 0.0 copy-start
  60.3 0.1 slice.15
  60.4 15.7 %collective-permute-start.8 = (bf16[128,2048]{1,0:T(8,128)(2,1)S(1)}, bf16[128,2048]{1,0:T(8,128)(2,1)S(1)}, u32[]{:S(2)}, u32[]{:S(2)}) collective-permute-start(bf16[128,2048]{1,0:T(8,128)(2,1)S(1)} %slice.15), channel_id=1, source_target_pairs={{0,4},{2,6},{4,0},{6,2},{8,12},{10,14},{12,8},{14,10},{16,20},{18,... | collective-permute-start | bytes 1572872 | tf_op jit(solution)/shard_map/ppermute | solution.py:287
  76.0 0.0 collective-permute-done.3
  76.0 13.6 %collective-permute-done.5 = bf16[576,512]{1,0:T(8,128)(2,1)S(1)} collective-permute-done((bf16[576,512]{1,0:T(8,128)(2,1)S(1)}, bf16[576,512]{1,0:T(8,128)(2,1)S(1)}, u32[]{:S(2)}, u32[]{:S(2)}) %collective-permute-start.5) | collective-permute-done | bytes 589856 | tf_op jit(solution)/shard_map/ppermute | solution.py:287
  89.6 0.0 copy-done
  89.6 0.2 fusion.1
  89.8 1.6 %collective-permute-start.6 = (bf16[576,512]{1,0:T(8,128)(2,1)S(1)}, bf16[576,512]{1,0:T(8,128)(2,1)S(1)}, u32[]{:S(2)}, u32[]{:S(2)}) collective-permute-start(bf16[576,512]{1,0:T(8,128)(2,1)S(1)} %fusion.1), channel_id=1, source_target_pairs={{0,1},{1,0},{2,3},{3,2},{4,5},{5,4},{6,7},{7,6},{8,9},{9,8},{10,11... | collective-permute-start | bytes 1769480 | tf_op jit(solution)/shard_map/ppermute | solution.py:321
  91.4 8.9 %collective-permute-done.8 = bf16[128,2048]{1,0:T(8,128)(2,1)S(1)} collective-permute-done((bf16[128,2048]{1,0:T(8,128)(2,1)S(1)}, bf16[128,2048]{1,0:T(8,128)(2,1)S(1)}, u32[]{:S(2)}, u32[]{:S(2)}) %collective-permute-start.8) | collective-permute-done | bytes 524320 | tf_op jit(solution)/shard_map/ppermute | solution.py:287
  100.3 0.9 fusion
  101.2 18.2 %all-to-all-start = ((bf16[4,32,2048]{2,1,0:T(8,128)(2,1)}), bf16[4,32,2048]{2,1,0:T(8,128)(2,1)S(1)}, u32[]{:S(2)}, u32[]{:S(2)}) async-start(bf16[4,32,2048]{2,1,0:T(8,128)(2,1)} %bitcast.4), calls=%async_computation | async-start | bytes 1048576 | tf_op jit(solution)/shard_map/all_to_all | solution.py:310
  119.4 0.0 collective-permute-done.6
  119.4 1.1 fusion.2
  120.5 13.3 %all-to-all-done = bf16[4,32,2048]{2,1,0:T(8,128)(2,1)S(1)} async-done(((bf16[4,32,2048]{2,1,0:T(8,128)(2,1)}), bf16[4,32,2048]{2,1,0:T(8,128)(2,1)S(1)}, u32[]{:S(2)}, u32[]{:S(2)}) %all-to-all-start) | async-done | bytes 524320 | tf_op jit(solution)/shard_map/all_to_all | solution.py:310
  133.9 0.8 convert_reduce_fusion
Async XLA Ops:
  0.6 17.7 %collective-permute-start = (bf16[576,512]{1,0:T(8,128)(2,1)}, bf16[576,512]{1,0:T(8,128)(2,1)S(1)}, u32[]{:S(2)}, u32[]{:S(2)}) collective-permute-start(bf16[576,512]{1,0:T(8,128)(2,1)} %bitcast.6), channel_id=1, source_target_pairs={{0,4},{2,6},{4,8},{6,10},{8,12},{10,14},{12,16},{14,18},{16,20},{1... | collective-permute-start | bytes 1769480 | tf_op jit(solution)/shard_map/ppermute | solution.py:287
  5.5 12.9 %collective-permute-start.2 = (bf16[576,512]{1,0:T(8,128)(2,1)}, bf16[576,512]{1,0:T(8,128)(2,1)S(1)}, u32[]{:S(2)}, u32[]{:S(2)}) collective-permute-start(bf16[576,512]{1,0:T(8,128)(2,1)} %bitcast.7), channel_id=1, source_target_pairs={{0,2},{2,8},{4,6},{6,12},{8,10},{10,16},{12,14},{14,20},{16,18},{1... | collective-permute-start | bytes 1769480 | tf_op jit(solution)/shard_map/ppermute | solution.py:287
  18.4 2.0 %copy-start.2 = (bf16[576,512]{1,0:T(8,128)(2,1)}, bf16[576,512]{1,0:T(8,128)(2,1)S(1)}, u32[]{:S(2)}) copy-start(bf16[576,512]{1,0:T(8,128)(2,1)S(1)} %collective-permute-done.refs_10_) | copy-start | bytes 1769476
  18.4 2.0 %collective-permute-start.1 = (bf16[576,512]{1,0:T(8,128)(2,1)S(1)}, bf16[576,512]{1,0:T(8,128)(2,1)S(1)}, u32[]{:S(2)}, u32[]{:S(2)}) collective-permute-start(bf16[576,512]{1,0:T(8,128)(2,1)S(1)} %collective-permute-done.refs_10_), channel_id=1, source_target_pairs={{0,2},{2,0},{4,6},{6,4},{8,10},{10,8},{12,14},{14,12},{16,18},{18,... | collective-permute-start | bytes 1769480 | tf_op jit(solution)/shard_map/ppermute | solution.py:287
  18.4 2.0 %copy-start.3 = (bf16[576,512]{1,0:T(8,128)(2,1)}, bf16[576,512]{1,0:T(8,128)(2,1)S(1)}, u32[]{:S(2)}) copy-start(bf16[576,512]{1,0:T(8,128)(2,1)S(1)} %collective-permute-done.2.refs_11_) | copy-start | bytes 1769476
  20.4 0.8 copy-start.4
  41.8 18.1 %copy-start.1 = (bf16[256,2048]{1,0:T(8,128)(2,1)S(1)}, bf16[256,2048]{1,0:T(8,128)(2,1)}, u32[]{:S(2)}) copy-start(bf16[256,2048]{1,0:T(8,128)(2,1)} %get-tuple-element.15) | copy-start | bytes 3145732
  41.8 18.1 %collective-permute-start.7 = (bf16[256,2048]{1,0:T(8,128)(2,1)}, bf16[256,2048]{1,0:T(8,128)(2,1)S(1)}, u32[]{:S(2)}, u32[]{:S(2)}) collective-permute-start(bf16[256,2048]{1,0:T(8,128)(2,1)} %get-tuple-element.16), channel_id=1, source_target_pairs={{0,2},{2,0},{4,6},{6,4},{8,10},{10,8},{12,14},{14,12},{16,18},{18,... | collective-permute-start | bytes 3145736 | tf_op jit(solution)/shard_map/ppermute | solution.py:287
  54.0 3.3 %collective-permute-start.4 = (bf16[576,512]{1,0:T(8,128)(2,1)}, bf16[576,512]{1,0:T(8,128)(2,1)S(1)}, u32[]{:S(2)}, u32[]{:S(2)}) collective-permute-start(bf16[576,512]{1,0:T(8,128)(2,1)} %get-tuple-element.14), channel_id=1, source_target_pairs={{0,2},{2,0},{4,6},{6,4},{8,10},{10,8},{12,14},{14,12},{16,18},{18,... | collective-permute-start | bytes 1769480 | tf_op jit(solution)/shard_map/ppermute | solution.py:287
  54.1 21.9 %collective-permute-start.3 = (bf16[576,512]{1,0:T(8,128)(2,1)}, bf16[576,512]{1,0:T(8,128)(2,1)S(1)}, u32[]{:S(2)}, u32[]{:S(2)}) collective-permute-start(bf16[576,512]{1,0:T(8,128)(2,1)} %get-tuple-element.12), channel_id=1, source_target_pairs={{2,0},{6,4},{8,2},{10,8},{12,6},{14,12},{16,10},{18,16},{20,14},{2... | collective-permute-start | bytes 1769480 | tf_op jit(solution)/shard_map/ppermute | solution.py:287
  58.6 31.0 %collective-permute-start.5 = (bf16[576,512]{1,0:T(8,128)(2,1)S(1)}, bf16[576,512]{1,0:T(8,128)(2,1)S(1)}, u32[]{:S(2)}, u32[]{:S(2)}) collective-permute-start(bf16[576,512]{1,0:T(8,128)(2,1)S(1)} %add_convert_fusion.1), channel_id=1, source_target_pairs={{4,0},{6,2},{8,4},{10,6},{12,8},{14,10},{16,12},{18,14},{20,16},{2... | collective-permute-start | bytes 1769480 | tf_op jit(solution)/shard_map/ppermute | solution.py:287
  60.3 29.3 %copy-start = (bf16[576,512]{1,0:T(8,128)(2,1)S(1)}, bf16[576,512]{1,0:T(8,128)(2,1)}, u32[]{:S(2)}) copy-start(bf16[576,512]{1,0:T(8,128)(2,1)} %get-tuple-element.11) | copy-start | bytes 1769476
  60.4 40.0 %collective-permute-start.8 = (bf16[128,2048]{1,0:T(8,128)(2,1)S(1)}, bf16[128,2048]{1,0:T(8,128)(2,1)S(1)}, u32[]{:S(2)}, u32[]{:S(2)}) collective-permute-start(bf16[128,2048]{1,0:T(8,128)(2,1)S(1)} %slice.15), channel_id=1, source_target_pairs={{0,4},{2,6},{4,0},{6,2},{8,12},{10,14},{12,8},{14,10},{16,20},{18,... | collective-permute-start | bytes 1572872 | tf_op jit(solution)/shard_map/ppermute | solution.py:287
  89.8 29.6 %collective-permute-start.6 = (bf16[576,512]{1,0:T(8,128)(2,1)S(1)}, bf16[576,512]{1,0:T(8,128)(2,1)S(1)}, u32[]{:S(2)}, u32[]{:S(2)}) collective-permute-start(bf16[576,512]{1,0:T(8,128)(2,1)S(1)} %fusion.1), channel_id=1, source_target_pairs={{0,1},{1,0},{2,3},{3,2},{4,5},{5,4},{6,7},{7,6},{8,9},{9,8},{10,11... | collective-permute-start | bytes 1769480 | tf_op jit(solution)/shard_map/ppermute | solution.py:321
  101.2 32.6 %all-to-all-start = ((bf16[4,32,2048]{2,1,0:T(8,128)(2,1)}), bf16[4,32,2048]{2,1,0:T(8,128)(2,1)S(1)}, u32[]{:S(2)}, u32[]{:S(2)}) async-start(bf16[4,32,2048]{2,1,0:T(8,128)(2,1)} %bitcast.4), calls=%async_computation | async-start | bytes 1048576 | tf_op jit(solution)/shard_map/all_to_all | solution.py:310

commit v3 on v2

v3 whole, which is shorter than its diff:
```python
import functools
import math

import jax
import jax.numpy as jnp
from jax import lax
from jax.experimental import pallas as pl
from jax.experimental.pallas import tpu as pltpu
from jax.sharding import PartitionSpec as P

NOPE = 128
ROPE = 64
VDIM = 128
LATENT = 512
REACH = 3
QK = NOPE + ROPE
KV = NOPE + VDIM
WIDTH = LATENT + ROPE
LANES = 128

MASKED = -1e30
FLOOR = -1e20
SCALE = 1.0 / math.sqrt(QK)
SCALE2 = SCALE * math.log2(math.e)

NT = (((1,), (1,)), ((), ()))
NN = (((1,), (0,)), ((), ()))


def dot(a, b, dims=NN):
    return lax.dot_general(a, b, dims, preferred_element_type=jnp.float32)


def head_cols(h, size):
    return slice(h * size, (h + 1) * size)


def score_block(h, latent, q_ref, do_ref, w_ref, bias, run_ref, keep):
    rows = q_ref.shape[0]
    lifted = dot(latent[:, :LATENT], w_ref[:, head_cols(h, KV)]).astype(jnp.bfloat16)
    key = jnp.concatenate([lifted[:, :NOPE], latent[:, LATENT:]], axis=1)
    raw = dot(key, q_ref[:, head_cols(h, QK)], NT)
    grads = dot(lifted[:, NOPE:], do_ref[:, head_cols(h, VDIM)], NT)
    for c in range(0, rows, LANES):
        cols = slice(c, c + LANES)
        scores = raw[:, cols] * SCALE2 + bias(cols)
        old_top = run_ref[h, 0:1, cols]
        new_top = jnp.maximum(old_top, jnp.max(scores, axis=0, keepdims=True))
        weights = jnp.exp2(scores - new_top)
        factor = jnp.exp2(old_top - new_top)
        run_ref[h, 0:1, cols] = new_top
        run_ref[h, 1:2, cols] = run_ref[h, 1:2, cols] * factor + jnp.sum(
            weights, axis=0, keepdims=True
        )
        run_ref[h, 2:3, cols] = run_ref[h, 2:3, cols] * factor + jnp.sum(
            weights * grads[:, cols], axis=0, keepdims=True
        )
        keep(cols, weights, grads[:, cols], new_top)
    return key


def grad_block(h, weights, grads, key, top, end_ref, q_t, do_t, dq_acc, first):
    rows = do_t.shape[1]
    factor = jnp.exp2(top - end_ref[h, 0:1, :]) * end_ref[h, 1:2, :]
    delta = end_ref[h, 2:3, :]
    lows, dscores = [], []
    for c in range(0, rows, LANES):
        cols = slice(c, c + LANES)
        probs = weights(cols) * factor[:, cols]
        lows.append(probs.astype(jnp.bfloat16))
        dscores.append((probs * (grads(cols) - delta[:, cols])).astype(jnp.bfloat16))
    low = jnp.concatenate(lows, axis=1)
    dscore = jnp.concatenate(dscores, axis=1)
    dvalue = dot(do_t[head_cols(h, VDIM), :], low, NT)
    dkey = dot(q_t[head_cols(h, QK), :], dscore, NT) * SCALE
    own = head_cols(h, QK)
    dq = dot(key.T, dscore)
    dq_acc[own, :] = dq + (first[own, :] if first is not None else dq_acc[own, :])
    columns = [dkey[:NOPE].astype(jnp.bfloat16), dvalue.astype(jnp.bfloat16)]
    return columns, dkey[NOPE:]


def start_stats(run_ref):
    rows = run_ref.shape[2]
    for h in range(2):
        run_ref[h, 0:1, :] = jnp.full((1, rows), FLOOR, jnp.float32)
        run_ref[h, 1:8, :] = jnp.zeros((7, rows), jnp.float32)


def own_score_kernel(
    index_ref, docs_ref, q_ref, do_ref, w_ref, lat_t_ref,
    e_ref, g_ref, k_ref, run_ref, lat_ref, bias_ref,
):
    rows = q_ref.shape[0]

    @pl.when(pl.program_id(0) == 0)
    def _():
        lat_ref[...] = lat_t_ref[...].T
        first_row = pl.multiple_of(index_ref[0] * rows, rows)
        docs = docs_ref[:, pl.ds(first_row, rows)]
        key_docs = jnp.broadcast_to(docs, (128, rows)).T[:, :1]
        key = lax.broadcasted_iota(jnp.int32, (rows, rows), 0)
        query = lax.broadcasted_iota(jnp.int32, (rows, rows), 1)
        bias_ref[...] = jnp.where((key_docs == docs) & (key <= query), 0.0, MASKED)

    start_stats(run_ref)
    for h in range(2):

        def keep(cols, weights, grads, new_top):
            e_ref[h, :, cols] = weights
            g_ref[h, :, cols] = grads

        k_ref[h, :, :] = score_block(
            h, lat_ref[...], q_ref, do_ref, w_ref, lambda cols: bias_ref[:, cols], run_ref, keep
        )


def earlier_kernel(
    index_ref, docs_sref, docs_ref, q_ref, do_ref, w_ref, own_run_ref, lat0, lat1, lat2,
    dq_ref, gw_ref, end_ref, x0_ref, x1_ref, x2_ref,
    lat_ref, lat_t_ref, bias_ref, e_ref, g_ref, k_ref, top_ref, run_ref, x_acc, sems,
):
    step = pl.program_id(0)
    rows = q_ref.shape[0]
    index = index_ref[0]
    odd = lax.rem(index, 2)
    first_row = index * rows
    first_doc = docs_sref[first_row]
    heads = range(2)

    def block_start(t):
        back = jnp.where(t == 1, 2, jnp.where(t == 0, 1 + 2 * odd, 3 - 2 * odd))
        return first_row - back * rows

    def active(t):
        start = block_start(t)
        return (start >= 0) & (docs_sref[jnp.maximum(start, 0) + rows - 1] >= first_doc)

    def block_rows(t):
        return pl.ds(pl.multiple_of(t * rows, rows), rows)

    def each_block(body):
        def visit(t, carry):
            @pl.when(active(t))
            def _():
                body(t)

            return carry

        lax.fori_loop(0, REACH, visit, 0)

    def fill_bias(t):
        my_docs = docs_ref[:, pl.ds(pl.multiple_of(first_row, rows), rows)]
        key_docs = docs_ref[:, pl.ds(pl.multiple_of(block_start(t), rows), rows)]
        key_docs = jnp.broadcast_to(key_docs, (128, rows)).T[:, :1]
        bias_ref[block_rows(t), :] = jnp.where(key_docs == my_docs, 0.0, MASKED)

    @pl.when(step == 0)
    def _():
        copies = [
            pltpu.make_async_copy(source, lat_t_ref.at[:, pl.ds(i * rows, rows)], sems.at[i])
            for i, source in enumerate((lat0, lat1, lat2))
        ]
        for copy in copies:
            copy.start()
        x_acc[...] = jnp.zeros_like(x_acc)
        each_block(fill_bias)
        for copy in copies:
            copy.wait()
        for i in range(REACH):
            part = slice(i * rows, (i + 1) * rows)
            lat_ref[part, :] = lat_t_ref[:, part].T

    gw_ref[...] = jnp.zeros_like(gw_ref)
    dq_ref[...] = jnp.zeros_like(dq_ref)
    run_ref[...] = own_run_ref[...]

    def first_pass(t):
        part = block_rows(t)
        latent = lat_ref[part, :]
        for h in heads:

            def keep(cols, weights, grads, new_top):
                e_ref[h, part, cols] = weights
                g_ref[h, part, cols] = grads
                top_ref[h, t, 0:1, cols] = new_top

            k_ref[h, part, :] = score_block(
                h, latent, q_ref, do_ref, w_ref, lambda cols: bias_ref[part, cols], run_ref, keep
            )

    each_block(first_pass)
    for h in heads:
        inverse = 1.0 / run_ref[h, 1:2, :]
        end_ref[h, 0:1, :] = run_ref[h, 0:1, :]
        end_ref[h, 1:2, :] = inverse
        end_ref[h, 2:3, :] = run_ref[h, 2:3, :] * inverse
        end_ref[h, 3:8, :] = jnp.zeros((5, rows), jnp.float32)
    q_t, do_t = q_ref[...].T, do_ref[...].T

    def second_pass(t):
        part = block_rows(t)
        columns, rope = [], 0.0
        for h in heads:
            made, turn = grad_block(
                h, lambda cols: e_ref[h, part, cols], lambda cols: g_ref[h, part, cols],
                k_ref[h, part, :], top_ref[h, t, 0:1, :], end_ref, q_t, do_t, dq_ref, None,
            )
            columns += made
            rope = rope + turn
        grads = jnp.concatenate(columns, axis=0)
        x_acc[:LATENT, part] += dot(w_ref[...], grads)
        x_acc[LATENT:, part] += rope
        gw_ref[...] += dot(lat_t_ref[:LATENT, part], grads, NT)

    each_block(second_pass)

    @pl.when(step == pl.num_programs(0) - 1)
    def _():
        for i, out in enumerate((x0_ref, x1_ref, x2_ref)):
            out[...] = x_acc[:, i * rows : (i + 1) * rows].astype(out.dtype)


def own_grad_kernel(
    ranks,
    index_ref, q_ref, do_ref, w_ref, lat_t_ref, e_ref, g_ref, k_ref, run_ref, end_ref,
    dq_in, gw_in, dq_ref, keep_ref, send_ref, x_ref, dq_acc, gw_acc, x_acc,
):
    step = pl.program_id(0)
    index = index_ref[0]

    @pl.when(step == 0)
    def _():
        x_acc[...] = jnp.zeros_like(x_acc)

    q_t, do_t = q_ref[...].T, do_ref[...].T
    columns = []
    for h in range(2):
        made, turn = grad_block(
            h, lambda cols: e_ref[h, :, cols], lambda cols: g_ref[h, :, cols],
            k_ref[h, :, :], run_ref[h, 0:1, :], end_ref, q_t, do_t, dq_acc, dq_in,
        )
        columns += made
        x_acc[LATENT:, :] += turn
    grads = jnp.concatenate(columns, axis=0)
    gw_acc[...] = gw_in[...] + dot(lat_t_ref[:LATENT, :], grads, NT)
    x_acc[:LATENT, :] += dot(w_ref[...], grads)
    dq_ref[...] = (dq_acc[...] * SCALE).T.astype(dq_ref.dtype)

    share, quarter = LATENT // ranks, LATENT // 4
    own_core, own_x = lax.rem(index, 2), lax.rem(index // 2, 2)
    for i in range(ranks // 4):
        for out, core in ((keep_ref, own_core), (send_ref, 1 - own_core)):
            for where, x in ((0, own_x), (quarter, 1 - own_x)):
                source = pl.multiple_of((4 * i + 2 * x + core) * share, share)
                out[where + i * share : where + (i + 1) * share, :] = gw_acc[
                    pl.ds(source, share), :
                ].astype(out.dtype)

    @pl.when(step == pl.num_programs(0) - 1)
    def _():
        x_ref[...] = x_acc[...].astype(x_ref.dtype)


def pair_cols(height, size):
    return pl.BlockSpec((height, 2 * size), lambda i: (0, i))


def pair_heads(*shape):
    return pl.BlockSpec((2, *shape), lambda i: (i, 0, 0))


def fixed(*shape):
    return pl.BlockSpec(shape, lambda i: (0, 0))


SCALARS = pl.BlockSpec(memory_space=pltpu.SMEM)


def call(body, pairs, flops, in_specs, out_specs, out_shape, scratch, name):
    return pl.pallas_call(
        body,
        grid=(pairs,),
        in_specs=in_specs,
        out_specs=out_specs,
        out_shape=[jax.ShapeDtypeStruct(shape, kind) for shape, kind in out_shape],
        scratch_shapes=scratch,
        compiler_params=pltpu.CompilerParams(
            dimension_semantics=("arbitrary",), vmem_limit_bytes=56 * 1024 * 1024
        ),
        cost_estimate=pl.CostEstimate(
            flops=flops, bytes_accessed=16 * 1024 * 1024, transcendentals=0
        ),
        name=name,
    )


def own_scores(index, docs, queries, grad_out, weight, latent):
    rows = queries.shape[0]
    pairs = weight.shape[1] // (2 * KV)
    low, full = jnp.bfloat16, jnp.float32
    return call(
        own_score_kernel,
        pairs,
        2 * pairs * rows * rows * 2 * (QK + VDIM + KV),
        [
            SCALARS, fixed(1, docs.shape[1]), pair_cols(rows, QK), pair_cols(rows, VDIM),
            pair_cols(LATENT, KV), fixed(WIDTH, rows),
        ],
        [pair_heads(rows, rows), pair_heads(rows, rows), pair_heads(rows, QK), pair_heads(8, rows)],
        [
            ((2 * pairs, rows, rows), full),
            ((2 * pairs, rows, rows), full),
            ((2 * pairs, rows, QK), low),
            ((2 * pairs, 8, rows), full),
        ],
        [pltpu.VMEM((rows, WIDTH), low), pltpu.VMEM((rows, rows), full)],
        "own_scores",
    )(index, docs, queries, grad_out, weight, latent)


def earlier_blocks(index, doc_ids, docs, queries, grad_out, weight, run, blocks):
    rows = queries.shape[0]
    pairs = weight.shape[1] // (2 * KV)
    window = REACH * rows
    low, full = jnp.bfloat16, jnp.float32
    return call(
        earlier_kernel,
        pairs,
        2 * pairs * rows * window * 2 * (3 * QK + 2 * VDIM + 3 * KV),
        [
            SCALARS, SCALARS, fixed(1, docs.shape[1]), pair_cols(rows, QK), pair_cols(rows, VDIM),
            pair_cols(LATENT, KV), pair_heads(8, rows),
        ]
        + [pl.BlockSpec(memory_space=pl.ANY)] * REACH,
        [
            pl.BlockSpec((2 * QK, rows), lambda i: (i, 0)), pair_cols(LATENT, KV),
            pair_heads(8, rows),
        ]
        + [fixed(WIDTH, rows)] * REACH,
        [
            ((pairs * 2 * QK, rows), full),
            ((LATENT, pairs * 2 * KV), full),
            ((2 * pairs, 8, rows), full),
        ]
        + [((WIDTH, rows), low)] * REACH,
        [
            pltpu.VMEM((window, WIDTH), low),
            pltpu.VMEM((WIDTH, window), low),
            pltpu.VMEM((window, rows), full),
            pltpu.VMEM((2, window, rows), full),
            pltpu.VMEM((2, window, rows), full),
            pltpu.VMEM((2, window, QK), low),
            pltpu.VMEM((2, REACH, 8, rows), full),
            pltpu.VMEM((2, 8, rows), full),
            pltpu.VMEM((WIDTH, window), full),
            pltpu.SemaphoreType.DMA((REACH,)),
        ],
        "earlier_blocks",
    )(index, doc_ids, docs, queries, grad_out, weight, run, *blocks)


def own_grads(index, queries, grad_out, weight, latent, kept, end, dq, gw, ranks):
    rows = queries.shape[0]
    pairs = weight.shape[1] // (2 * KV)
    low, full = jnp.bfloat16, jnp.float32
    half = pair_cols(LATENT // 2, KV)
    return call(
        functools.partial(own_grad_kernel, ranks),
        pairs,
        2 * pairs * rows * rows * 2 * (2 * QK + VDIM + 2 * KV),
        [
            SCALARS, pair_cols(rows, QK), pair_cols(rows, VDIM), pair_cols(LATENT, KV),
            fixed(WIDTH, rows), pair_heads(rows, rows), pair_heads(rows, rows),
            pair_heads(rows, QK), pair_heads(8, rows), pair_heads(8, rows),
            pl.BlockSpec((2 * QK, rows), lambda i: (i, 0)), pair_cols(LATENT, KV),
        ],
        [pair_cols(rows, QK), half, half, fixed(WIDTH, rows)],
        [
            (queries.shape, low),
            ((LATENT // 2, pairs * 2 * KV), low),
            ((LATENT // 2, pairs * 2 * KV), low),
            ((WIDTH, rows), low),
        ],
        [
            pltpu.VMEM((2 * QK, rows), full),
            pltpu.VMEM((LATENT, 2 * KV), full),
            pltpu.VMEM((WIDTH, rows), full),
        ],
        "own_grads",
    )(index, queries, grad_out, weight, latent, *kept, end, dq, gw)


def permute(value, axis, target):
    count = lax.axis_size(axis)
    pairs = [(s, target(s)) for s in range(count) if 0 <= target(s) < count]
    return lax.ppermute(value, axis, pairs)


def local(kv_latent, queries, grad_out, kv_up_weight, doc_ids):
    ranks = lax.axis_size("ctx")
    index = lax.axis_index("ctx").astype(jnp.int32)[None]
    low, full = jnp.bfloat16, jnp.float32
    docs = doc_ids[None]

    latent = kv_latent.T
    far = permute(latent, "ctx", lambda s: s + 2)
    mixed = permute(latent, "ctx", lambda s: s + 3 if s % 2 else s + 1)
    *kept, run = own_scores(index, docs, queries, grad_out, kv_up_weight, latent)
    far, run = lax.optimization_barrier((far, run))
    swapped = permute(far, "ctx", lambda s: s ^ 1)

    dq, gw, end, to_swap, to_far, to_mixed = earlier_blocks(
        index, doc_ids, docs, queries, grad_out, kv_up_weight, run, (swapped, far, mixed)
    )
    from_mixed = permute(to_mixed, "ctx", lambda s: s - 1 if s % 2 else s - 3)
    from_swap = permute(to_swap, "ctx", lambda s: s ^ 1)
    far_sum = (to_far.astype(full) + from_swap.astype(full)).astype(low)
    far_sum, gw = lax.optimization_barrier((far_sum, gw))
    from_far = permute(far_sum, "ctx", lambda s: s - 2)
    grad_queries, keep, send, mine = own_grads(
        index, queries, grad_out, kv_up_weight, latent, (*kept, run), end, dq, gw, ranks
    )

    from_far, from_mixed, send = lax.optimization_barrier((from_far, from_mixed, send))

    chip = keep.astype(full) + permute(send, "ctx", lambda s: s ^ 1).astype(full)
    quarter = LATENT // 4
    from_x = permute(chip[quarter:].astype(low), "ctx", lambda s: s ^ 2)
    plane = (chip[:quarter] + from_x.astype(full)).astype(low)
    columns = [list(range(first, ranks, 4)) for first in range(4)]
    pieces = lax.all_to_all(plane, "ctx", 0, 0, axis_index_groups=columns, tiled=True)
    grad_weight = jnp.sum(pieces.reshape(ranks // 4, LATENT // ranks, -1).astype(full), axis=0)

    total = mine.astype(full) + from_mixed.astype(full) + from_far.astype(full)
    mine = total.astype(low)
    size = lax.axis_size("head")
    for turn in range(1, size):
        other = lax.ppermute(mine, "head", [(s, (s + turn) % size) for s in range(size)])
        total = total + other.astype(full)
    return grad_queries, total.astype(low).T, grad_weight


def solution(mesh):
    return jax.shard_map(
        local,
        mesh=mesh,
        in_specs=(P("ctx", None), P("ctx", "head"), P("ctx", "head"), P(None, "head"), P()),
        out_specs=(P("ctx", "head"), P("ctx", None), P("ctx", "head")),
        check_vma=False,
    )
```

time: 135 us -> 133 us (0.985)
  Pallas kernels: 20.6 us -> 36.5 us
  waiting for transfers between devices: 51.1 us -> 40.7 us
  starting transfers between devices: 56.7 us -> 48.1 us
    pallas_call x1 -> x3, Pallas kernels: 20.6 us -> 36.5 us  [the longest x1 15.9 us: own_grads(): call(functools.partial(own_grad_kernel, ranks), pairs, 2 * pairs * rows *...]
    ppermute x8, waiting for transfers between devices: 37.8 us -> 27.8 us  [permute(): return lax.ppermute(value, axis, pairs)]
    ppermute x8, starting transfers between devices: 36.9 us -> 29.7 us  [permute(): return lax.ppermute(value, axis, pairs)]
    all_to_all x1, starting transfers between devices: 18.2 us -> 16.8 us  [local(): lax.all_to_all(plane, 'ctx', 0, 0, axis_index_groups=columns, tiled=True)]
  transfers between devices with their start and end apart: 10 -> 10, of which waited for: 6 -> 7; matrix products, arithmetic and copies ran while one was open for 3% -> 3% of each run, Pallas kernels for 0% -> 20%
where the time goes in v3:
time: 133 us
  starting transfers between devices  48.1 us (36%)
  waiting for transfers between devices  40.7 us (31%)
  Pallas kernels  36.5 us (27%)
  other arithmetic  5.83 us (4%)
    ppermute x8, starting transfers between devices, permute(): return lax.ppermute(value, axis, pairs)  29.7 us
    ppermute x8, waiting for transfers between devices, permute(): return lax.ppermute(value, axis, pairs)  27.8 us
    all_to_all x1, starting transfers between devices, local(): lax.all_to_all(plane, 'ctx', 0, 0, axis_index_groups=columns, tiled=True)  16.8 us
    pallas_call x1, Pallas kernels, own_grads(): call(functools.partial(own_grad_kernel, ranks), pairs, 2 * pairs * rows *...  15.9 us
    all_to_all x1, waiting for transfers between devices, local(): lax.all_to_all(plane, 'ctx', 0, 0, axis_index_groups=columns, tiled=True)  12.8 us
    pallas_call x1, Pallas kernels, own_scores(): call(own_score_kernel, pairs, 2 * pairs * rows * rows * 2 * (QK + VDIM +...  11.2 us
    pallas_call x1, Pallas kernels, earlier_blocks(): call(earlier_kernel, pairs, 2 * pairs * rows * window * 2 * (3 * QK + 2 *...  9.43 us
  transfers between devices with their start and end apart: 10, of which 7 were waited for; matrix products, arithmetic and copies ran while one was open for 3% of the time, Pallas kernels for 20%

profile of v3, /device:TPU:0, one launch (start us, length us, event | category | flops | bytes accessed | tf_op | source)
XLA Modules:
  0.0 132.7 jit_solution(332913004750856488)
XLA Ops:
  0.6 4.9 %collective-permute-start = (bf16[576,512]{1,0:T(8,128)(2,1)}, bf16[576,512]{1,0:T(8,128)(2,1)S(1)}, u32[]{:S(2)}, u32[]{:S(2)}) collective-permute-start(bf16[576,512]{1,0:T(8,128)(2,1)} %bitcast.6), channel_id=1, source_target_pairs={{0,4},{2,6},{4,8},{6,10},{8,12},{10,14},{12,16},{14,18},{16,20},{1... | collective-permute-start | bytes 1769480 | tf_op jit(solution)/shard_map/ppermute | solution.py:397
  5.5 1.5 %collective-permute-start.2 = (bf16[576,512]{1,0:T(8,128)(2,1)}, bf16[576,512]{1,0:T(8,128)(2,1)S(1)}, u32[]{:S(2)}, u32[]{:S(2)}) collective-permute-start(bf16[576,512]{1,0:T(8,128)(2,1)} %bitcast.7), channel_id=1, source_target_pairs={{0,2},{2,8},{4,6},{6,12},{8,10},{10,16},{12,14},{14,20},{16,18},{1... | collective-permute-start | bytes 1769480 | tf_op jit(solution)/shard_map/ppermute | solution.py:397
  7.0 11.2 %own_scores.1 = (f32[8,512,512]{2,1,0:T(8,128)}, f32[8,512,512]{2,1,0:T(8,128)}, bf16[8,512,192]{2,1,0:T(8,128)(2,1)}, f32[8,8,512]{2,1,0:T(8,128)}) custom-call(s32[1]{0:T(128)} %bitcast.index_ref, s32[1,8192]{1,0:T(1,128)} %bitcast.10, bf16[512,1536]{1,0:T(8,128)(2,1)} %q_ref.5, bf16[512,1024]{1,0:T(8,128)(2,1)} %do_ref.5, bf16[512,2048]{1,0:T(8,128)(2,1)} %w_ref.5, ...), custom_call_target="tpu_custom_call" | custom-call | flops 2415919104 | bytes 16777216 | tf_op jit(solution)/shard_map/own_scores/pallas_call | solution.py:302
  18.2 0.1 collective-permute-done.lat1
  18.4 0.0 copy-start.1
  18.4 2.0 %collective-permute-start.1 = (bf16[576,512]{1,0:T(8,128)(2,1)S(1)}, bf16[576,512]{1,0:T(8,128)(2,1)S(1)}, u32[]{:S(2)}, u32[]{:S(2)}) collective-permute-start(bf16[576,512]{1,0:T(8,128)(2,1)S(1)} %collective-permute-done.lat1), channel_id=1, source_target_pairs={{0,2},{2,0},{4,6},{6,4},{8,10},{10,8},{12,14},{14,12},{16,18},{18,... | collective-permute-start | bytes 1769480 | tf_op jit(solution)/shard_map/ppermute | solution.py:397
  20.4 0.0 collective-permute-done.2.lat2
  20.4 0.0 copy-start.2
  20.4 1.6 %collective-permute-done.1.lat0 = bf16[576,512]{1,0:T(8,128)(2,1)S(1)} collective-permute-done((bf16[576,512]{1,0:T(8,128)(2,1)S(1)}, bf16[576,512]{1,0:T(8,128)(2,1)S(1)}, u32[]{:S(2)}, u32[]{:S(2)}) %collective-permute-start.1) | collective-permute-done | bytes 589856 | tf_op jit(solution)/shard_map/ppermute | solution.py:397
  22.0 0.0 copy-done.1
  22.0 0.0 copy-done.2
  22.0 0.0 copy-start.3
  22.0 0.8 copy-done.3
  22.8 9.4 %earlier_blocks.1 = (f32[1536,512]{1,0:T(8,128)}, f32[512,2048]{1,0:T(8,128)}, f32[8,8,512]{2,1,0:T(8,128)}, bf16[576,512]{1,0:T(8,128)(2,1)}, bf16[576,512]{1,0:T(8,128)(2,1)}, /*index=5*/bf16[576,512]{1,0:T(8,128)(2,1)}) custom-call(s32[1]{0:T(128)} %bitcast.index_ref, s32[8192]{0:T(1024)} %docs_sref.1, s32[1,8192]{1,0:T(1,128)} %bitcast.11, ...), custom_call_target="tpu_custom_call" | custom-call | flops 20132659200 | bytes 16777216 | tf_op jit(solution)/shard_map/earlier_blocks/pallas_call | solution.py:327
  32.3 10.5 %collective-permute-start.3 = (bf16[576,512]{1,0:T(8,128)(2,1)}, bf16[576,512]{1,0:T(8,128)(2,1)S(1)}, u32[]{:S(2)}, u32[]{:S(2)}) collective-permute-start(bf16[576,512]{1,0:T(8,128)(2,1)} %get-tuple-element.33), channel_id=1, source_target_pairs={{0,2},{2,0},{4,6},{6,4},{8,10},{10,8},{12,14},{14,12},{16,18},{18,... | collective-permute-start | bytes 1769480 | tf_op jit(solution)/shard_map/ppermute | solution.py:397
  42.7 1.3 collective-permute-start.5
  44.0 0.6 collective-permute-done.3
  44.6 1.2 add_convert_fusion.1
  45.8 1.3 collective-permute-start.4
  47.1 15.9 %own_grads.1 = (bf16[512,1536]{1,0:T(8,128)(2,1)}, bf16[256,2048]{1,0:T(8,128)(2,1)}, bf16[256,2048]{1,0:T(8,128)(2,1)}, bf16[576,512]{1,0:T(8,128)(2,1)}) custom-call(s32[1]{0:T(128)} %bitcast.index_ref, bf16[512,1536]{1,0:T(8,128)(2,1)} %q_ref.5, bf16[512,1024]{1,0:T(8,128)(2,1)} %do_ref.5, bf16[512,2048]{1,0:T(8,128)(2,1)} %w_ref.5, ...), custom_call_target="tpu_custom_call" | custom-call | flops 4294967296 | bytes 16777216 | tf_op jit(solution)/shard_map/own_grads/pallas_call | solution.py:368
  63.0 0.0 collective-permute-done.5
  63.0 12.0 %collective-permute-done.4 = bf16[576,512]{1,0:T(8,128)(2,1)S(1)} collective-permute-done((bf16[576,512]{1,0:T(8,128)(2,1)S(1)}, bf16[576,512]{1,0:T(8,128)(2,1)S(1)}, u32[]{:S(2)}, u32[]{:S(2)}) %collective-permute-start.4) | collective-permute-done | bytes 589856 | tf_op jit(solution)/shard_map/ppermute | solution.py:397
  75.0 0.0 collective-permute-start.7
  75.0 2.9 %collective-permute-done.7 = bf16[256,2048]{1,0:T(8,128)(2,1)S(1)} collective-permute-done((bf16[256,2048]{1,0:T(8,128)(2,1)}, bf16[256,2048]{1,0:T(8,128)(2,1)S(1)}, u32[]{:S(2)}, u32[]{:S(2)}) %collective-permute-start.7) | collective-permute-done | bytes 1048608 | tf_op jit(solution)/shard_map/ppermute | solution.py:397
  77.8 1.6 %convert_add_fusion = f32[256,2048]{1,0:T(8,128)S(1)} fusion(bf16[256,2048]{1,0:T(8,128)(2,1)S(1)} %collective-permute-done.7, bf16[256,2048]{1,0:T(8,128)(2,1)} %get-tuple-element.43), kind=kLoop, calls=%fused_computation | loop fusion | flops 1572864 | bytes 4194304 | tf_op jit(solution)/shard_map/add | solution.py:427
  79.4 0.0 copy-start
  79.4 0.1 slice.15
  79.5 8.3 %collective-permute-start.8 = (bf16[128,2048]{1,0:T(8,128)(2,1)S(1)}, bf16[128,2048]{1,0:T(8,128)(2,1)S(1)}, u32[]{:S(2)}, u32[]{:S(2)}) collective-permute-start(bf16[128,2048]{1,0:T(8,128)(2,1)S(1)} %slice.15), channel_id=1, source_target_pairs={{0,4},{2,6},{4,0},{6,2},{8,12},{10,14},{12,8},{14,10},{16,20},{18,... | collective-permute-start | bytes 1572872 | tf_op jit(solution)/shard_map/ppermute | solution.py:397
  87.8 0.0 copy-done
  87.8 0.2 fusion.1
  88.0 1.6 %collective-permute-start.6 = (bf16[576,512]{1,0:T(8,128)(2,1)S(1)}, bf16[576,512]{1,0:T(8,128)(2,1)S(1)}, u32[]{:S(2)}, u32[]{:S(2)}) collective-permute-start(bf16[576,512]{1,0:T(8,128)(2,1)S(1)} %fusion.1), channel_id=1, source_target_pairs={{0,1},{1,0},{2,3},{3,2},{4,5},{5,4},{6,7},{7,6},{8,9},{9,8},{10,11... | collective-permute-start | bytes 1769480 | tf_op jit(solution)/shard_map/ppermute | solution.py:439
  89.6 10.6 %collective-permute-done.8 = bf16[128,2048]{1,0:T(8,128)(2,1)S(1)} collective-permute-done((bf16[128,2048]{1,0:T(8,128)(2,1)S(1)}, bf16[128,2048]{1,0:T(8,128)(2,1)S(1)}, u32[]{:S(2)}, u32[]{:S(2)}) %collective-permute-start.8) | collective-permute-done | bytes 524320 | tf_op jit(solution)/shard_map/ppermute | solution.py:397
  100.2 0.9 fusion
  101.2 16.8 %all-to-all-start = ((bf16[4,32,2048]{2,1,0:T(8,128)(2,1)}), bf16[4,32,2048]{2,1,0:T(8,128)(2,1)S(1)}, u32[]{:S(2)}, u32[]{:S(2)}) async-start(bf16[4,32,2048]{2,1,0:T(8,128)(2,1)} %bitcast.4), calls=%async_computation | async-start | bytes 1048576 | tf_op jit(solution)/shard_map/all_to_all | solution.py:432
  118.0 0.0 collective-permute-done.6
  118.0 1.1 fusion.2
  119.1 12.8 %all-to-all-done = bf16[4,32,2048]{2,1,0:T(8,128)(2,1)S(1)} async-done(((bf16[4,32,2048]{2,1,0:T(8,128)(2,1)}), bf16[4,32,2048]{2,1,0:T(8,128)(2,1)S(1)}, u32[]{:S(2)}, u32[]{:S(2)}) %all-to-all-start) | async-done | bytes 524320 | tf_op jit(solution)/shard_map/all_to_all | solution.py:432
  131.9 0.8 convert_reduce_fusion
Async XLA Ops:
  0.6 17.7 %collective-permute-start = (bf16[576,512]{1,0:T(8,128)(2,1)}, bf16[576,512]{1,0:T(8,128)(2,1)S(1)}, u32[]{:S(2)}, u32[]{:S(2)}) collective-permute-start(bf16[576,512]{1,0:T(8,128)(2,1)} %bitcast.6), channel_id=1, source_target_pairs={{0,4},{2,6},{4,8},{6,10},{8,12},{10,14},{12,16},{14,18},{16,20},{1... | collective-permute-start | bytes 1769480 | tf_op jit(solution)/shard_map/ppermute | solution.py:397
  5.5 14.9 %collective-permute-start.2 = (bf16[576,512]{1,0:T(8,128)(2,1)}, bf16[576,512]{1,0:T(8,128)(2,1)S(1)}, u32[]{:S(2)}, u32[]{:S(2)}) collective-permute-start(bf16[576,512]{1,0:T(8,128)(2,1)} %bitcast.7), channel_id=1, source_target_pairs={{0,2},{2,8},{4,6},{6,12},{8,10},{10,16},{12,14},{14,20},{16,18},{1... | collective-permute-start | bytes 1769480 | tf_op jit(solution)/shard_map/ppermute | solution.py:397
  18.4 3.6 %copy-start.1 = (bf16[576,512]{1,0:T(8,128)(2,1)}, bf16[576,512]{1,0:T(8,128)(2,1)S(1)}, u32[]{:S(2)}) copy-start(bf16[576,512]{1,0:T(8,128)(2,1)S(1)} %collective-permute-done.lat1) | copy-start | bytes 1769476
  18.4 3.6 %collective-permute-start.1 = (bf16[576,512]{1,0:T(8,128)(2,1)S(1)}, bf16[576,512]{1,0:T(8,128)(2,1)S(1)}, u32[]{:S(2)}, u32[]{:S(2)}) collective-permute-start(bf16[576,512]{1,0:T(8,128)(2,1)S(1)} %collective-permute-done.lat1), channel_id=1, source_target_pairs={{0,2},{2,0},{4,6},{6,4},{8,10},{10,8},{12,14},{14,12},{16,18},{18,... | collective-permute-start | bytes 1769480 | tf_op jit(solution)/shard_map/ppermute | solution.py:397
  20.4 1.6 %copy-start.2 = (bf16[576,512]{1,0:T(8,128)(2,1)}, bf16[576,512]{1,0:T(8,128)(2,1)S(1)}, u32[]{:S(2)}) copy-start(bf16[576,512]{1,0:T(8,128)(2,1)S(1)} %collective-permute-done.2.lat2) | copy-start | bytes 1769476
  22.0 0.8 copy-start.3
  32.3 12.3 %collective-permute-start.3 = (bf16[576,512]{1,0:T(8,128)(2,1)}, bf16[576,512]{1,0:T(8,128)(2,1)S(1)}, u32[]{:S(2)}, u32[]{:S(2)}) collective-permute-start(bf16[576,512]{1,0:T(8,128)(2,1)} %get-tuple-element.33), channel_id=1, source_target_pairs={{0,2},{2,0},{4,6},{6,4},{8,10},{10,8},{12,14},{14,12},{16,18},{18,... | collective-permute-start | bytes 1769480 | tf_op jit(solution)/shard_map/ppermute | solution.py:397
  42.7 20.2 %collective-permute-start.5 = (bf16[576,512]{1,0:T(8,128)(2,1)}, bf16[576,512]{1,0:T(8,128)(2,1)S(1)}, u32[]{:S(2)}, u32[]{:S(2)}) collective-permute-start(bf16[576,512]{1,0:T(8,128)(2,1)} %get-tuple-element.39), channel_id=1, source_target_pairs={{2,0},{6,4},{8,2},{10,8},{12,6},{14,12},{16,10},{18,16},{20,14},{2... | collective-permute-start | bytes 1769480 | tf_op jit(solution)/shard_map/ppermute | solution.py:397
  45.8 29.2 %collective-permute-start.4 = (bf16[576,512]{1,0:T(8,128)(2,1)S(1)}, bf16[576,512]{1,0:T(8,128)(2,1)S(1)}, u32[]{:S(2)}, u32[]{:S(2)}) collective-permute-start(bf16[576,512]{1,0:T(8,128)(2,1)S(1)} %add_convert_fusion.1), channel_id=1, source_target_pairs={{4,0},{6,2},{8,4},{10,6},{12,8},{14,10},{16,12},{18,14},{20,16},{2... | collective-permute-start | bytes 1769480 | tf_op jit(solution)/shard_map/ppermute | solution.py:397
  75.0 2.9 %collective-permute-start.7 = (bf16[256,2048]{1,0:T(8,128)(2,1)}, bf16[256,2048]{1,0:T(8,128)(2,1)S(1)}, u32[]{:S(2)}, u32[]{:S(2)}) collective-permute-start(bf16[256,2048]{1,0:T(8,128)(2,1)} %get-tuple-element.44), channel_id=1, source_target_pairs={{0,2},{2,0},{4,6},{6,4},{8,10},{10,8},{12,14},{14,12},{16,18},{18,... | collective-permute-start | bytes 3145736 | tf_op jit(solution)/shard_map/ppermute | solution.py:397
  79.4 8.4 %copy-start = (bf16[576,512]{1,0:T(8,128)(2,1)S(1)}, bf16[576,512]{1,0:T(8,128)(2,1)}, u32[]{:S(2)}) copy-start(bf16[576,512]{1,0:T(8,128)(2,1)} %get-tuple-element.37) | copy-start | bytes 1769476
  79.5 20.8 %collective-permute-start.8 = (bf16[128,2048]{1,0:T(8,128)(2,1)S(1)}, bf16[128,2048]{1,0:T(8,128)(2,1)S(1)}, u32[]{:S(2)}, u32[]{:S(2)}) collective-permute-start(bf16[128,2048]{1,0:T(8,128)(2,1)S(1)} %slice.15), channel_id=1, source_target_pairs={{0,4},{2,6},{4,0},{6,2},{8,12},{10,14},{12,8},{14,10},{16,20},{18,... | collective-permute-start | bytes 1572872 | tf_op jit(solution)/shard_map/ppermute | solution.py:397
  88.0 30.0 %collective-permute-start.6 = (bf16[576,512]{1,0:T(8,128)(2,1)S(1)}, bf16[576,512]{1,0:T(8,128)(2,1)S(1)}, u32[]{:S(2)}, u32[]{:S(2)}) collective-permute-start(bf16[576,512]{1,0:T(8,128)(2,1)S(1)} %fusion.1), channel_id=1, source_target_pairs={{0,1},{1,0},{2,3},{3,2},{4,5},{5,4},{6,7},{7,6},{8,9},{9,8},{10,11... | collective-permute-start | bytes 1769480 | tf_op jit(solution)/shard_map/ppermute | solution.py:439
  101.2 30.8 %all-to-all-start = ((bf16[4,32,2048]{2,1,0:T(8,128)(2,1)}), bf16[4,32,2048]{2,1,0:T(8,128)(2,1)S(1)}, u32[]{:S(2)}, u32[]{:S(2)}) async-start(bf16[4,32,2048]{2,1,0:T(8,128)(2,1)} %bitcast.4), calls=%async_computation | async-start | bytes 1048576 | tf_op jit(solution)/shard_map/all_to_all | solution.py:432
